TPU v7x, 256 devices: a whole 4x4x8 slice. The times are simulated.
256 devices in a mesh: vox: 16 (over z, core), dir: 16 (over x, y).
Axes of the slice: x: 4, y: 4, z: 8, core: 2. Of those that a mesh axis runs over, the one named last changes fastest.
Arguments:
- signals: bfloat16 [1152, 2, 4, 2048], P('dir', None, None, 'vox'), may hold values from -6 to 6
- basis: float32 [1152, 45], P('dir'), may hold values from -0.1875 to 0.1875
- response: float32 [3, 5], replicated, may hold values from 0.1 to 1
- shell_index: int32 [1152], P('dir'), may hold values from 0 to 2
- brain_mask: int32 [2, 4, 2048], P(None, None, 'vox'), may hold values 0 or 1
- fodf: float32 [45, 2, 4, 2048], P(None, None, None, 'vox'), may hold values from -4 to 4
- aux_field: float32 [45, 2, 2, 4, 2048], P(None, None, None, None, 'vox'), may hold values from -2.4 to 2.4
- grad_dual: float32 [45, 2, 2, 4, 2048], P(None, None, None, None, 'vox'), may hold values from -0.8 to 0.8
- sym_dual: float32 [45, 3, 2, 4, 2048], P(None, None, None, None, 'vox'), may hold values from -0.8 to 0.8
- data_dual: float32 [1152, 2, 4, 2048], P('dir', None, None, 'vox'), may hold values from -3 to 3
Outputs:
- fodf_out: float32 [45, 2, 4, 2048], P(None, None, None, 'vox')
- aux_out: float32 [45, 2, 2, 4, 2048], P(None, None, None, None, 'vox')
All inputs are finite; a program needn't handle non-finite values. No bound on the sum of `brain_mask` on one device may be relied on, other than what follows from the above.
Results may differ from a plain program's by a relative error of at most 0.0003.
Values sent between devices are 32-bit elements; how exact they have to be, the bound alone decides.
A program may use at most 64 MiB of HBM per device.

v0:
```python
import jax
import jax.numpy as jnp
import numpy as np
from jax import lax
from jax.sharding import PartitionSpec as P

ITERS = 2


sigma_step = 0.25
tau_step = 0.3
alpha_one = 1.0
alpha_zero = 1.5
order_table = np.repeat(np.arange(5), [1, 5, 9, 13, 17]).astype(np.int32)
highest = lax.Precision.HIGHEST


def shifted(x, axis, by):
    length = lax.axis_size(axis)
    pairs = [(i, i + by) for i in range(length) if 0 <= i + by < length]
    return lax.ppermute(x, axis, pairs)


def build_kernel(basis, response, shell_index):
    nshell, norder = response.shape
    shell_hot = (shell_index[:, None] == lax.broadcasted_iota(jnp.int32, (1, nshell), 1)).astype(
        jnp.float32
    )
    per_order = jnp.dot(shell_hot, response, precision=highest)
    order_hot = (
        jnp.asarray(order_table)[None, :] == lax.broadcasted_iota(jnp.int32, (norder, 1), 0)
    ).astype(jnp.float32)
    return basis * jnp.dot(per_order, order_hot, precision=highest)


def rows_forward(field):
    step = field[..., 1:, :] - field[..., :-1, :]
    return jnp.concatenate([step, jnp.zeros_like(field[..., :1, :])], -2)


def rows_backward(field):
    count = field.shape[-2]
    keep = (lax.broadcasted_iota(jnp.int32, (count, 1), 0) < count - 1).astype(field.dtype)
    prior = jnp.concatenate([jnp.zeros_like(field[..., :1, :]), field[..., :-1, :]], -2)
    return field * keep - prior


def cols_forward(field, ahead, keep_next):
    upcoming = jnp.concatenate([field[..., 1:], ahead], -1)
    return (upcoming - field) * keep_next


def cols_backward(field, behind, keep_next):
    prior = jnp.concatenate([behind, field[..., :-1]], -1)
    return field * keep_next - prior


def from_right(edge):
    return shifted(edge, "vox", -1)


def from_left(edge):
    return shifted(edge, "vox", 1)


def plain_norms(p_sq, q_sq):
    return (p_sq, q_sq)


def dual_update(ubar, wbar, p_cur, q_cur, keep_next, reduce_norms):
    ahead = from_right(ubar[..., :1])
    behind = from_left(wbar[..., -1:])
    grad_u = jnp.stack([rows_forward(ubar), cols_forward(ubar, ahead, keep_next)], 1)
    p_tilde = p_cur + sigma_step * (grad_u - wbar)
    e_rows = rows_backward(wbar[:, 0])
    e_cols = cols_backward(wbar[:, 1], behind[:, 1], keep_next)
    e_mixed = 0.5 * (cols_backward(wbar[:, 0], behind[:, 0], keep_next) + rows_backward(wbar[:, 1]))
    q_tilde = q_cur + sigma_step * jnp.stack([e_rows, e_cols, e_mixed], 1)
    p_sq = jnp.sum(p_tilde * p_tilde, axis=(0, 1))
    q_sq = jnp.sum(q_tilde[:, 0] ** 2 + q_tilde[:, 1] ** 2 + 2.0 * q_tilde[:, 2] ** 2, axis=0)
    p_sq, q_sq = reduce_norms(p_sq, q_sq)
    p_new = p_tilde / jnp.maximum(1.0, jnp.sqrt(p_sq) / alpha_one)
    q_new = q_tilde / jnp.maximum(1.0, jnp.sqrt(q_sq) / alpha_zero)
    return (p_new, q_new)


def primal_update(u_cur, w_cur, p_new, q_new, adjoint, keep_next):
    behind = from_left(p_new[:, 1, ..., -1:])
    ahead = from_right(q_new[:, 1:, ..., :1])
    div_p = rows_backward(p_new[:, 0]) + cols_backward(p_new[:, 1], behind, keep_next)
    u_next = u_cur - tau_step * (adjoint - div_p)
    div_rows = rows_forward(q_new[:, 0]) + cols_forward(q_new[:, 2], ahead[:, 1], keep_next)
    div_cols = cols_forward(q_new[:, 1], ahead[:, 0], keep_next) + rows_forward(q_new[:, 2])
    w_next = w_cur + tau_step * (p_new + jnp.stack([div_rows, div_cols], 1))
    return (u_next, w_next)


def data_update(kernel, ubar, dual_flat, sig_flat, mask_flat):
    predicted = jnp.dot(kernel, ubar.reshape(ubar.shape[0], -1), precision=highest)
    return mask_flat * (dual_flat + sigma_step * (predicted - sig_flat)) / (1.0 + sigma_step)


def body(
    signals,
    basis,
    response,
    shell_index,
    brain_mask,
    fodf,
    aux_field,
    grad_dual,
    sym_dual,
    data_dual,
):
    ncoef, planes, rows, cols = fodf.shape
    total_cols = cols * lax.axis_size("vox")
    col_ids = lax.axis_index("vox") * cols + lax.broadcasted_iota(jnp.int32, (cols,), 0)
    keep_next = (col_ids < total_cols - 1).astype(jnp.float32)
    kernel = build_kernel(basis, response, shell_index)
    mask_flat = brain_mask.reshape(1, -1).astype(jnp.float32)
    sig_flat = signals.reshape(signals.shape[0], -1).astype(jnp.float32)
    dual_flat = data_dual.reshape(data_dual.shape[0], -1)
    u_cur, w_cur, p_cur, q_cur = (fodf, aux_field, grad_dual, sym_dual)
    ubar, wbar = (fodf, aux_field)
    for step in range(ITERS):
        p_cur, q_cur = dual_update(ubar, wbar, p_cur, q_cur, keep_next, plain_norms)
        dual_flat = data_update(kernel, ubar, dual_flat, sig_flat, mask_flat)
        partial_adj = lax.dot_general(
            kernel, dual_flat, (((0,), (0,)), ((), ())), precision=highest
        )
        adjoint = lax.psum(partial_adj, "dir").reshape(fodf.shape)
        u_next, w_next = primal_update(u_cur, w_cur, p_cur, q_cur, adjoint, keep_next)
        ubar = 2.0 * u_next - u_cur
        wbar = 2.0 * w_next - w_cur
        u_cur, w_cur = (u_next, w_next)
    return (u_cur, w_cur)


def solution(mesh):
    placed = (
        P("dir", None, None, "vox"),
        P("dir", None),
        P(),
        P("dir"),
        P(None, None, "vox"),
        P(None, None, None, "vox"),
        P(None, None, None, None, "vox"),
        P(None, None, None, None, "vox"),
        P(None, None, None, None, "vox"),
        P("dir", None, None, "vox"),
    )
    return jax.shard_map(
        body,
        mesh=mesh,
        in_specs=placed,
        out_specs=(P(None, None, None, "vox"), P(None, None, None, None, "vox")),
        check_vma=False,
    )
```

profile of v0, /device:TPU:96, one launch (start us, length us, event | category | flops | bytes accessed | tf_op | source)
XLA Modules:
  0.0 216.2 jit_solution(10066316138110997342)
XLA Ops:
  7.2 1.1 reshape.85
  13.3 1.9 collective-permute-start
  15.6 2.7 %collective-permute-done = f32[45,2,4,1]{3,2,1,0:T(4,128)S(1)} collective-permute-done((f32[45,2,4,1]{3,2,1,0:T(4,128)S(1)}, f32[45,2,4,1]{3,2,1,0:T(4,128)S(1)}, u32[]{:S(2)}, u32[]{:S(2)}) %collective-permute-start) | collective-permute-done | bytes 1472 | tf_op jit(solution)/shard_map/ppermute | solution.py:21
  18.5 1.0 multiply_reduce_fusion.1
  19.8 5.3 %collective-permute-start.3 = (f32[45,2,2,4,1]{4,3,2,0,1:T(4,128)S(1)}, f32[45,2,2,4,1]{4,3,2,0,1:T(4,128)S(1)}, u32[]{:S(2)}, u32[]{:S(2)}) collective-permute-start(f32[45,2,2,4,1]{4,3,2,0,1:T(4,128)S(1)} %slice.282), channel_id=1, source_target_pairs={{0,16},{16,32},{32,48},{48,64},{64,80},{80,96},{96,112},{112,128},... | collective-permute-start | bytes 8648 | tf_op jit(solution)/shard_map/ppermute | solution.py:21
  25.7 3.1 %collective-permute-done.3 = f32[45,2,2,4,1]{4,3,2,0,1:T(4,128)S(1)} collective-permute-done((f32[45,2,2,4,1]{4,3,2,0,1:T(4,128)S(1)}, f32[45,2,2,4,1]{4,3,2,0,1:T(4,128)S(1)}, u32[]{:S(2)}, u32[]{:S(2)}) %collective-permute-start.3) | collective-permute-done | bytes 2912 | tf_op jit(solution)/shard_map/ppermute | solution.py:21
  31.1 1.9 collective-permute-start.4
  33.4 4.6 %collective-permute-done.4 = f32[45,2,2,4,1]{4,3,2,0,1:T(4,128)S(1)} collective-permute-done((f32[45,2,2,4,1]{4,3,2,0,1:T(4,128)S(1)}, f32[45,2,2,4,1]{4,3,2,0,1:T(4,128)S(1)}, u32[]{:S(2)}, u32[]{:S(2)}) %collective-permute-start.4) | collective-permute-done | bytes 2912 | tf_op jit(solution)/shard_map/ppermute | solution.py:21
  38.8 1.6 copy.69
  40.4 1.5 copy.70
  41.9 1.6 copy.71
  43.6 1.5 copy.72
  45.1 1.4 fusion.37
  49.1 1.0 slice.311
  50.1 1.6 copy.61
  51.7 6.5 %collective-permute-start.1 = (f32[45,2,4,1]{0,2,3,1:T(4,128)}, f32[45,2,4,1]{0,2,3,1:T(4,128)}, u32[]{:S(2)}, u32[]{:S(2)}) collective-permute-start(f32[45,2,4,1]{0,2,3,1:T(4,128)} %bitcast.144), channel_id=1, source_target_pairs={{0,16},{16,32},{32,48},{48,64},{64,80},{80,96},{96,112},{112,128},... | collective-permute-start | bytes 4328 | tf_op jit(solution)/shard_map/ppermute | solution.py:21
  58.3 1.9 collective-permute-start.6
  60.9 1.5 copy.62
  62.4 5.0 %collective-permute-done.6 = f32[45,2,2,4,1]{4,3,2,1,0:T(4,128)} collective-permute-done((f32[45,2,2,4,1]{4,3,2,1,0:T(4,128)}, f32[45,2,2,4,1]{4,3,2,1,0:T(4,128)}, u32[]{:S(2)}, u32[]{:S(2)}) %collective-permute-start.6) | collective-permute-done | bytes 2912 | tf_op jit(solution)/shard_map/ppermute | solution.py:21
  67.4 1.8 slice_bitcast_fusion.4
  69.2 1.7 copy.80
  70.8 1.5 copy.81
  72.3 1.8 maximum_subtract_fusion.10
  74.1 34.8 %all-reduce.15.cloned.1.call-done = f32[45,2,4,128]{3,2,1,0:T(4,128)} async-done(((f32[45,2,4,128]{3,2,1,0:T(4,128)}), f32[45,2,4,128]{3,2,1,0:T(4,128)}) %all-reduce.15.cloned.1.call-update) | async-done | bytes 184336 | tf_op jit(solution)/shard_map/psum | solution.py:131
  109.5 2.2 %multiply_subtract_fusion.1 = (f32[45,2,4,128]{3,2,1,0:T(4,128)S(1)}, f32[45,2,4,128]{3,2,1,0:T(4,128)}) fusion(f32[45,2,4,128]{3,2,1,0:T(4,128)S(1)} %copy-done.2, f32[45,2,4,128]{3,2,1,0:T(4,128)} %all-reduce.15.cloned.1.call-done, f32[45,2,4,127]{3,2,1,0:T(4,128)} %bitcast.134, f32[45,2,4,1]{3,2,1,0:T(4,128)} %copy.62, f32[128]{0:T(128)S(1)} %compare_convert_fusion.1, ...), kind=kLoop, calls=%fused_computation.113 | loop fusion | flops 506880 | bytes 1429008 | tf_op jit(solution)/shard_map/sub | solution.py:133
  114.9 1.9 collective-permute-start.2
  117.0 2.8 %collective-permute-done.2 = f32[45,2,4,1]{3,2,1,0:T(4,128)S(1)} collective-permute-done((f32[45,2,4,1]{3,2,1,0:T(4,128)S(1)}, f32[45,2,4,1]{3,2,1,0:T(4,128)S(1)}, u32[]{:S(2)}, u32[]{:S(2)}) %collective-permute-start.2) | collective-permute-done | bytes 1472 | tf_op jit(solution)/shard_map/ppermute | solution.py:21
  123.2 3.8 %collective-permute-start.7 = (f32[45,2,2,4,1]{4,3,2,0,1:T(4,128)S(1)}, f32[45,2,2,4,1]{4,3,2,0,1:T(4,128)S(1)}, u32[]{:S(2)}, u32[]{:S(2)}) collective-permute-start(f32[45,2,2,4,1]{4,3,2,0,1:T(4,128)S(1)} %slice.325), channel_id=1, source_target_pairs={{16,0},{32,16},{48,32},{64,48},{80,64},{96,80},{112,96},{128,112},... | collective-permute-start | bytes 8648 | tf_op jit(solution)/shard_map/ppermute | solution.py:21
  127.5 4.6 %collective-permute-done.7 = f32[45,2,2,4,1]{4,3,2,0,1:T(4,128)S(1)} collective-permute-done((f32[45,2,2,4,1]{4,3,2,0,1:T(4,128)S(1)}, f32[45,2,2,4,1]{4,3,2,0,1:T(4,128)S(1)}, u32[]{:S(2)}, u32[]{:S(2)}) %collective-permute-start.7) | collective-permute-done | bytes 2912 | tf_op jit(solution)/shard_map/ppermute | solution.py:21
  133.5 6.2 %collective-permute-start.5 = (f32[45,2,4,1]{0,2,3,1:T(4,128)S(1)}, f32[45,2,4,1]{0,2,3,1:T(4,128)S(1)}, u32[]{:S(2)}, u32[]{:S(2)}) collective-permute-start(f32[45,2,4,1]{0,2,3,1:T(4,128)S(1)} %bitcast.143), channel_id=1, source_target_pairs={{0,16},{16,32},{32,48},{48,64},{64,80},{80,96},{96,112},{112,128},... | collective-permute-start | bytes 4328 | tf_op jit(solution)/shard_map/ppermute | solution.py:21
  140.9 66.6 %all-reduce.17.cloned.1.call-done = f32[45,2,4,128]{3,2,1,0:T(4,128)} async-done(((f32[45,2,4,128]{3,2,1,0:T(4,128)}), f32[45,2,4,128]{3,2,1,0:T(4,128)}) %all-reduce.17.cloned.1.call-update) | async-done | bytes 184336 | tf_op jit(solution)/shard_map/psum | solution.py:131
  207.5 1.9 fusion.44
  (127 shorter events, 23.3 us)
Async XLA Ops:
  7.2 2.8 %copy-start = (f32[3,5]{1,0:T(4,128)S(1)}, f32[3,5]{1,0:T(4,128)}, u32[]{:S(2)}) copy-start(f32[3,5]{1,0:T(4,128)} %param.13) | copy-start | bytes 184
  7.2 1.2 copy-start.15
  7.2 101.7 %all-reduce.15.cloned.1.call-start = ((), (), s32[]{:S(2)}) async-start(), calls=%async_computation | async-start | bytes 368640 | tf_op jit(solution)/shard_map/psum | solution.py:131
  8.4 0.9 copy-start.2
  9.3 0.7 copy-start.20
  10.0 0.7 copy-start.22
  10.6 0.7 copy-start.21
  10.6 0.7 copy-start.23
  13.3 194.2 %all-reduce.17.cloned.1.call-start = ((), (), s32[]{:S(2)}) async-start(), calls=%async_computation.1 | async-start | bytes 368640 | tf_op jit(solution)/shard_map/psum | solution.py:131
  13.3 5.0 %collective-permute-start = (f32[45,2,4,1]{3,2,1,0:T(4,128)S(1)}, f32[45,2,4,1]{3,2,1,0:T(4,128)S(1)}, u32[]{:S(2)}, u32[]{:S(2)}) collective-permute-start(f32[45,2,4,1]{3,2,1,0:T(4,128)S(1)} %bitcast.123), channel_id=1, source_target_pairs={{16,0},{32,16},{48,32},{64,48},{80,64},{96,80},{112,96},{128,112},... | collective-permute-start | bytes 4328 | tf_op jit(solution)/shard_map/ppermute | solution.py:21
  15.3 14.0 %copy-start.17 = (f32[4]{0:T(128)}, f32[4]{0:T(128)S(1)}, u32[]{:S(2)}) copy-start(f32[4]{0:T(128)S(1)} %compare_convert_fusion) | copy-start | bytes 52
  15.6 2.9 %copy-start.3 = (f32[45,2,2,4,128]{4,3,2,1,0:T(4,128)S(1)}, f32[45,2,2,4,128]{4,3,2,1,0:T(4,128)}, u32[]{:S(2)}) copy-start(f32[45,2,2,4,128]{4,3,2,1,0:T(4,128)} %param.17) | copy-start | bytes 1105924
  15.6 2.9 %copy-start.14 = (f32[45,2,2,4,128]{4,3,2,1,0:T(4,128)S(1)}, f32[45,2,2,4,128]{4,3,2,1,0:T(4,128)}, u32[]{:S(2)}) copy-start(f32[45,2,2,4,128]{4,3,2,1,0:T(4,128)} %param.18) | copy-start | bytes 1105924
  19.8 9.0 %collective-permute-start.3 = (f32[45,2,2,4,1]{4,3,2,0,1:T(4,128)S(1)}, f32[45,2,2,4,1]{4,3,2,0,1:T(4,128)S(1)}, u32[]{:S(2)}, u32[]{:S(2)}) collective-permute-start(f32[45,2,2,4,1]{4,3,2,0,1:T(4,128)S(1)} %slice.282), channel_id=1, source_target_pairs={{0,16},{16,32},{32,48},{48,64},{64,80},{80,96},{96,112},{112,128},... | collective-permute-start | bytes 8648 | tf_op jit(solution)/shard_map/ppermute | solution.py:21
  29.3 1.1 copy-start.1
  31.1 6.9 %collective-permute-start.4 = (f32[45,2,2,4,1]{4,3,2,0,1:T(4,128)S(1)}, f32[45,2,2,4,1]{4,3,2,0,1:T(4,128)S(1)}, u32[]{:S(2)}, u32[]{:S(2)}) collective-permute-start(f32[45,2,2,4,1]{4,3,2,0,1:T(4,128)S(1)} %slice.296), channel_id=1, source_target_pairs={{16,0},{32,16},{48,32},{64,48},{80,64},{96,80},{112,96},{128,112},... | collective-permute-start | bytes 8648 | tf_op jit(solution)/shard_map/ppermute | solution.py:21
  45.1 1.4 copy-start.7
  46.4 0.7 copy-start.16
  49.1 11.1 %copy-start.4 = (f32[45,2,4,128]{3,2,1,0:T(4,128)}, f32[45,2,4,128]{3,2,1,0:T(4,128)S(1)}, u32[]{:S(2)}) copy-start(f32[45,2,4,128]{3,2,1,0:T(4,128)S(1)} %slice_bitcast_fusion.15) | copy-start | bytes 552964
  51.7 9.1 %collective-permute-start.1 = (f32[45,2,4,1]{0,2,3,1:T(4,128)}, f32[45,2,4,1]{0,2,3,1:T(4,128)}, u32[]{:S(2)}, u32[]{:S(2)}) collective-permute-start(f32[45,2,4,1]{0,2,3,1:T(4,128)} %bitcast.144), channel_id=1, source_target_pairs={{0,16},{16,32},{32,48},{48,64},{64,80},{80,96},{96,112},{112,128},... | collective-permute-start | bytes 4328 | tf_op jit(solution)/shard_map/ppermute | solution.py:21
  58.3 9.1 %collective-permute-start.6 = (f32[45,2,2,4,1]{4,3,2,1,0:T(4,128)}, f32[45,2,2,4,1]{4,3,2,1,0:T(4,128)}, u32[]{:S(2)}, u32[]{:S(2)}) collective-permute-start(f32[45,2,2,4,1]{4,3,2,1,0:T(4,128)} %slice.311), channel_id=1, source_target_pairs={{0,16},{16,32},{32,48},{48,64},{64,80},{80,96},{96,112},{112,128},... | collective-permute-start | bytes 8648 | tf_op jit(solution)/shard_map/ppermute | solution.py:21
  69.2 3.2 %copy-start.11 = (f32[45,1,2,4,127]{4,3,2,0,1:T(4,128)S(1)}, f32[45,1,2,4,127]{4,3,2,0,1:T(4,128)}, u32[]{:S(2)}) copy-start(f32[45,1,2,4,127]{4,3,2,0,1:T(4,128)} %slice_bitcast_fusion.3) | copy-start | bytes 548644
  112.4 0.9 copy-start.8
  112.4 0.9 copy-start.13
  114.9 5.0 %collective-permute-start.2 = (f32[45,2,4,1]{3,2,1,0:T(4,128)S(1)}, f32[45,2,4,1]{3,2,1,0:T(4,128)S(1)}, u32[]{:S(2)}, u32[]{:S(2)}) collective-permute-start(f32[45,2,4,1]{3,2,1,0:T(4,128)S(1)} %bitcast.124), channel_id=1, source_target_pairs={{16,0},{32,16},{48,32},{64,48},{80,64},{96,80},{112,96},{128,112},... | collective-permute-start | bytes 4328 | tf_op jit(solution)/shard_map/ppermute | solution.py:21
  120.3 0.9 copy-start.5
  120.3 1.0 copy-start.10
  120.4 1.0 copy-start.19
  121.3 0.9 copy-start.6
  123.2 8.8 %collective-permute-start.7 = (f32[45,2,2,4,1]{4,3,2,0,1:T(4,128)S(1)}, f32[45,2,2,4,1]{4,3,2,0,1:T(4,128)S(1)}, u32[]{:S(2)}, u32[]{:S(2)}) collective-permute-start(f32[45,2,2,4,1]{4,3,2,0,1:T(4,128)S(1)} %slice.325), channel_id=1, source_target_pairs={{16,0},{32,16},{48,32},{64,48},{80,64},{96,80},{112,96},{128,112},... | collective-permute-start | bytes 8648 | tf_op jit(solution)/shard_map/ppermute | solution.py:21
  133.5 7.2 %collective-permute-start.5 = (f32[45,2,4,1]{0,2,3,1:T(4,128)S(1)}, f32[45,2,4,1]{0,2,3,1:T(4,128)S(1)}, u32[]{:S(2)}, u32[]{:S(2)}) collective-permute-start(f32[45,2,4,1]{0,2,3,1:T(4,128)S(1)} %bitcast.143), channel_id=1, source_target_pairs={{0,16},{16,32},{32,48},{48,64},{64,80},{80,96},{96,112},{112,128},... | collective-permute-start | bytes 4328 | tf_op jit(solution)/shard_map/ppermute | solution.py:21
  140.7 66.8 %copy-start.9 = (f32[45,2,4,128]{3,2,1,0:T(4,128)S(1)}, f32[45,2,4,128]{3,2,1,0:T(4,128)}, u32[]{:S(2)}) copy-start(f32[45,2,4,128]{3,2,1,0:T(4,128)} %get-tuple-element.9) | copy-start | bytes 552964
  (2 other events, 1.2 us)
Sparse Core Ops, SparseCore 0:
  13.4 95.4 all-reduce.14
  115.0 92.3 all-reduce.16
where the time goes:
time: 218 us; the launch traced here: 216 us
  waiting for transfers between devices  124 us (57%)
  local copies, waits for them, and re-layouts  32.3 us (15%)
  starting transfers between devices  29.6 us (14%)
  between operations  14.6 us (7%)
  other arithmetic  13.5 us (6%)
    psum x2, waiting for transfers between devices, body(): adjoint = lax.psum(partial_adj, 'dir').reshape(fodf.shape)  101 us
    ppermute x8, starting transfers between devices, shifted(): return lax.ppermute(x, axis, pairs)  29.5 us
    ppermute x8, waiting for transfers between devices, shifted(): return lax.ppermute(x, axis, pairs)  22.8 us
    unnamed x48, local copies, waits for them, and re-layouts  7.32 us
  transfers between devices with their start and end apart: 10, of which 8 were waited for; matrix products, arithmetic and copies ran while one was open for 14% of the time, Pallas kernels for 0%

commit v1 on v0

v1 whole, which is shorter than its diff:
```python
import functools

import jax
import jax.numpy as jnp
import numpy as np
from jax import lax
from jax.experimental import pallas as pl
from jax.experimental.pallas import tpu as pltpu
from jax.sharding import PartitionSpec as P

MESH = pl.DeviceIdType.MESH
f32 = jnp.float32
bf16 = jnp.bfloat16

SIGMA = 0.25
TAU = 0.3
ALPHA1 = 1.0
ALPHA0 = 1.5
ORDER_STARTS = (1, 6, 15, 28)

NC = 45
CP = 48
HALF = 24
ND = 72
NR = 8
SIDE = 4


def split(x):
    hi = x.astype(bf16)
    return hi, (x - hi.astype(f32)).astype(bf16)


def mm(a, b):
    return jnp.dot(a, b, preferred_element_type=f32)


def mm3(ah, al, x):
    xh, xl = split(x)
    return mm(ah, xh) + mm(ah, xl) + mm(al, xh)


def rows_of(pr):
    start = pr * CP
    return pl.ds(start if isinstance(start, int) else pl.multiple_of(start, 8), CP)


def kernel(
    nvox,
    sig_hbm, basis_hbm, resp_hbm, shell_hbm, mask_hbm, fodf_hbm, aux_hbm, grad_hbm, sym_hbm, dual_hbm,
    u_hbm, w_hbm,
    sig, basis, resp, shell, mask, u0, w0, p0, q0, y0, sigf,
    kt, ta, tb, fa, fb, ra, rb, hg,
    halo, halo_l, halo_r, edge, edge_l, edge_r, edge_c, edge_in, wk,
    p1r, p1c, q1a, q1b, q1c, wbr, wbc, w1r, w1c, pbr, pbc, ub, v2r, v2c, u1, ub1, gu, p2r, p2c,
    uo, wo,
    in_sem, out_sem, sa_s, sa_r, sb_s, sb_r, ga_s, ga_r, gb_s, gb_r, ec_s, ec_r, vox_s, vox_r,
):
    me = lax.axis_index("dir")
    vox = lax.axis_index("vox")
    mx, my = me // SIDE, lax.rem(me, SIDE)
    npeer = SIDE * SIDE
    order = sorted(range(1, npeer), key=lambda k: -(min(k // SIDE, SIDE - k // SIDE) + min(k % SIDE, SIDE - k % SIDE)))

    def peer(k):
        return lax.rem(mx + k // SIDE, SIDE) * SIDE + lax.rem(my + k % SIDE, SIDE)

    def source(k):
        return lax.rem(mx + SIDE - k // SIDE, SIDE) * SIDE + lax.rem(my + SIDE - k % SIDE, SIDE)

    right, left = lax.rem(vox + 1, nvox), lax.rem(vox + nvox - 1, nvox)

    def load(i, src, dst):
        return pltpu.make_async_copy(src, dst, in_sem.at[i])

    loads = [
        load(0, basis_hbm, basis),
        load(1, resp_hbm, resp),
        load(2, shell_hbm, shell),
        load(3, mask_hbm, mask),
        load(4, fodf_hbm, u0.at[pl.ds(0, NC * NR)]),
        load(5, sig_hbm, sig),
        load(6, dual_hbm, y0),
        load(7, aux_hbm, w0.at[pl.ds(0, NC * 2 * NR)]),
        load(8, grad_hbm, p0.at[pl.ds(0, NC * 2 * NR)]),
        load(9, sym_hbm, q0.at[pl.ds(0, NC * 3 * NR)]),
    ]
    for c in loads:
        c.start()

    barrier = pltpu.get_barrier_semaphore()
    for k in order:
        pl.semaphore_signal(barrier, inc=1, device_id={"dir": peer(k)}, device_id_type=MESH)
    for n in (left, right):
        pl.semaphore_signal(barrier, inc=1, device_id={"vox": n}, device_id_type=MESH)

    lane = lax.broadcasted_iota(jnp.int32, (1, 128), 1)
    for ref, n in ((u0, 1), (w0, 2), (p0, 2), (q0, 3)):
        ref[pl.ds(NC * n * NR, (CP - NC) * n * NR), :] = jnp.zeros(((CP - NC) * n * NR, 128), f32)

    for c in loads[:3]:
        c.wait()
    kt[...] = jnp.zeros((CP, 128), f32)
    sh = shell[...]
    per_order = [
        jnp.where(sh == 0, resp[0:1, o : o + 1], jnp.where(sh == 1, resp[1:2, o : o + 1], resp[2:3, o : o + 1]))
        for o in range(5)
    ]
    cid = lax.broadcasted_iota(jnp.int32, (NC, 1), 0)
    scale = jnp.broadcast_to(per_order[0], (NC, ND))
    for o, start in enumerate(ORDER_STARTS):
        scale = jnp.where(cid >= start, per_order[o + 1], scale)
    kt[pl.ds(0, NC), pl.ds(0, ND)] = basis[...] * scale
    ktv = kt[...]
    knv = jnp.concatenate([ktv, jnp.zeros((128 - CP, 128), f32)], 0).T[0:ND]
    kth, ktl = split(ktv[:, 0:ND])
    knh128, knl128 = split(knv)
    knh, knl = knh128[:, 0:CP], knl128[:, 0:CP]

    for c in loads[3:7]:
        c.wait()

    def to_f32(i, _):
        at = pl.ds(pl.multiple_of(i * 96, 96), 96)
        sigf[at, :] = sig[at, :].astype(f32)
        return 0

    lax.fori_loop(0, 6, to_f32, 0)

    def natural(ref, pr, n, comp, count):
        return ref[pl.ds(comp * NR + pr, count, stride=n * NR), :]

    def pair(ref, i, count):
        return jnp.concatenate([natural(ref, 2 * i, 1, 0, count), natural(ref, 2 * i + 1, 1, 0, count)], 1)

    def store_pair(ref, i, val):
        ref[rows_of(2 * i), :] = val[:, 0:128]
        ref[rows_of(2 * i + 1), :] = val[:, 128:256]

    def data_step(i, _):
        pred = mm3(knh, knl, pair(u0, i, CP))
        m = jnp.concatenate([mask[pl.ds(2 * i, 1), :], mask[pl.ds(2 * i + 1, 1), :]], 1).astype(f32)
        y = (m * (1.0 / (1.0 + SIGMA))) * (pair(y0, i, ND) + SIGMA * (pred - pair(sigf, i, ND)))
        store_pair(ta, i, mm3(kth, ktl, y))
        return 0

    lax.fori_loop(0, 4, data_step, 0)

    def chunk(d):
        return pl.ds(pl.multiple_of(d * HALF, HALF), HALF)

    def scatter(src, dst, ss, rs, k):
        return pltpu.make_async_remote_copy(
            src_ref=src.at[chunk(peer(k))], dst_ref=dst.at[k], send_sem=ss.at[k], recv_sem=rs.at[k],
            device_id={"dir": peer(k)}, device_id_type=MESH)

    def gather(ref, ss, rs, k, at):
        return pltpu.make_async_remote_copy(
            src_ref=ref.at[chunk(at)], dst_ref=ref.at[chunk(at)], send_sem=ss.at[k], recv_sem=rs.at[k],
            device_id={"dir": peer(k)}, device_id_type=MESH)

    def to_vox(src, dst, n, k):
        return pltpu.make_async_remote_copy(
            src_ref=src, dst_ref=dst, send_sem=vox_s.at[k], recv_sem=vox_r.at[k],
            device_id={"vox": n}, device_id_type=MESH)

    pl.semaphore_wait(barrier, npeer - 1 + 2)
    send_a = [scatter(ta, ra, sa_s, sa_r, k) for k in order]
    for c in send_a:
        c.start()

    slot_of = lane // 8
    j = lax.rem(lane, 8)

    def pack_into(acc, val, pr):
        for h in range(2):
            s = h * NR + pr
            t = pltpu.roll(val[h * HALF : (h + 1) * HALF], 8 * s + 2 if isinstance(s, int) and 8 * s + 2 < 128 else lax.rem(8 * s + 2, 128), 1)
            acc = jnp.where(slot_of == s, t, acc)
        return acc

    zero24 = jnp.zeros((HALF, 128), f32)
    edge[...] = lax.fori_loop(0, NR, lambda pr, acc: pack_into(acc, ta[rows_of(pr), :], pr), zero24)
    edge_right, edge_left = to_vox(edge, edge_l, right, 0), to_vox(edge, edge_r, left, 1)
    edge_right.start()
    edge_left.start()

    def signal_step(i, _):
        s = pair(sigf, i, ND).astype(bf16)
        store_pair(tb, i, mm(kth, s) + mm(ktl, s))
        return 0

    lax.fori_loop(0, 4, signal_step, 0)
    gram = mm3(kth, ktl, knv)
    hpart = gram[0:HALF] + pltpu.roll(gram[HALF:CP], 64, 1)
    for pr in range(NR):
        tb[pl.ds(pr * CP + NC, CP - NC), :] = hpart[3 * pr : 3 * pr + 3]
    send_b = [scatter(tb, rb, sb_s, sb_r, k) for k in order]
    for c in send_b:
        c.start()

    for c in loads[7:]:
        c.wait()

    fields = ((u0, 1, 0), (w0, 2, 0), (w0, 2, 1), (p0, 2, 0), (p0, 2, 1), (q0, 3, 0), (q0, 3, 1), (q0, 3, 2))

    def pack_step(pr, accs):
        return tuple(pack_into(acc, natural(ref, pr, n, comp, CP), pr) for acc, (ref, n, comp) in zip(accs, fields))

    packed = lax.fori_loop(0, NR, pack_step, (zero24,) * 8)
    for f in range(8):
        halo[pl.ds(f * HALF, HALF), :] = packed[f]
    halo_right, halo_left = to_vox(halo, halo_l, right, 2), to_vox(halo, halo_r, left, 3)
    halo_right.start()
    halo_left.start()

    def reduce_chunk(src, scattered, recv, full):
        total = src[chunk(me), :]
        for c, k in zip(scattered, order):
            c.wait_recv()
            total = total + recv[k]
        full[chunk(me), :] = total

    reduce_chunk(ta, send_a, ra, fa)
    give_a = [gather(fa, ga_s, ga_r, k, me) for k in order]
    for c in give_a:
        c.start()

    has_left = vox > 0
    has_right = vox < nvox - 1
    edge_right.wait_recv()
    edge_left.wait_recv()
    near = jnp.where((j == 1) & has_left, edge_l[...], 0.0) + jnp.where((j == 6) & has_right, pltpu.roll(edge_r[...], 4, 1), 0.0)
    edge_c[...] = near[0:8] + pltpu.roll(near[8:16], 1, 1) + pltpu.roll(near[16:24], 2, 1)

    def spread(k):
        return pltpu.make_async_remote_copy(
            src_ref=edge_c, dst_ref=edge_in.at[k], send_sem=ec_s.at[k], recv_sem=ec_r.at[k],
            device_id={"dir": peer(k)}, device_id_type=MESH)

    send_e = [spread(k) for k in order]
    for c in send_e:
        c.start()

    halo_right.wait_recv()
    halo_left.wait_recv()

    def widen(f):
        at = pl.ds(f * HALF, HALF)
        own = halo[at, :]
        far_l = jnp.where(has_left, halo_l[at, :], 0.0)
        far_r = jnp.where(has_right, halo_r[at, :], 0.0)
        return jnp.where(j < 2, far_l, jnp.where(j < 4, own, pltpu.roll(jnp.where(j < 2, own, far_r), 4, 1)))

    col = jnp.where(j < 4, j - 2, j + 122) + vox * 128
    keep_w = ((col >= 0) & (col < nvox * 128 - 1)).astype(f32)
    rid = lax.rem(lane // 8, 4)
    low_w, high_w = (rid < 3).astype(f32), (rid >= 1).astype(f32)

    def fr_w(x):
        return (pltpu.roll(x, 120, 1) - x) * low_w

    def br_w(x):
        return x * low_w - pltpu.roll(x, 8, 1) * high_w

    def fx_w(x):
        return (pltpu.roll(x, 127, 1) - x) * keep_w

    def bx_w(x):
        return x * keep_w - pltpu.roll(x, 1, 1)

    def shrink(sq, alpha):
        return jnp.minimum(1.0, alpha * lax.rsqrt(sq))

    def norm_w(sq):
        n = jnp.sum(sq, 0, keepdims=True)
        return n + pltpu.roll(n, 64, 1)

    def dual_p_w(pr_, pc_, u_, wr_, wc_):
        a = pr_ + SIGMA * (fr_w(u_) - wr_)
        b = pc_ + SIGMA * (fx_w(u_) - wc_)
        s = shrink(norm_w(a * a + b * b), ALPHA1)
        return a * s, b * s

    def dual_q_w(qa_, qb_, qc_, wr_, wc_):
        a = qa_ + SIGMA * br_w(wr_)
        b = qb_ + SIGMA * bx_w(wc_)
        c = qc_ + (0.5 * SIGMA) * (bx_w(wr_) + br_w(wc_))
        s = shrink(norm_w(a * a + b * b + 2.0 * (c * c)), ALPHA0)
        return a * s, b * s, c * s

    uw, wrw, wcw = widen(0), widen(1), widen(2)
    p1rw, p1cw = dual_p_w(widen(3), widen(4), uw, wrw, wcw)
    q1aw, q1bw, q1cw = dual_q_w(widen(5), widen(6), widen(7), wrw, wcw)
    w1rw = wrw + TAU * (p1rw + fr_w(q1aw) + fx_w(q1cw))
    w1cw = wcw + TAU * (p1cw + fx_w(q1bw) + fr_w(q1cw))
    wbrw, wbcw = 2.0 * w1rw - wrw, 2.0 * w1cw - wcw
    _, q2bw, q2cw = dual_q_w(q1aw, q1bw, q1cw, wbrw, wbcw)
    pbrw, pbcw = p1rw - SIGMA * wbrw, p1cw - SIGMA * wbcw
    ubw = uw + TAU * (br_w(p1rw) + bx_w(p1cw))
    for n, val in enumerate((uw, wrw, wcw, p1cw, q1bw, q1cw, wbrw, wbcw, q2bw, q2cw, pbrw, pbcw, ubw)):
        wk[n] = val

    keep = jnp.where(lane + vox * 128 < nvox * 128 - 1, 1.0, 0.0).astype(f32)

    def beside(val, pr, at):
        parts = [pltpu.roll(val, at - 8 * (h * NR + pr), 1) for h in range(2)]
        return jnp.concatenate(parts, 0)

    def nxt(x, far, pr):
        return jnp.where(lane == 127, beside(far, pr, 121), pltpu.roll(x, 127, 1))

    def prv(x, far, pr):
        return jnp.where(lane == 0, beside(far, pr, 127), pltpu.roll(x, 1, 1))

    def fx(x, far, pr):
        return (nxt(x, far, pr) - x) * keep

    def bx(x, far, pr):
        return x * keep - prv(x, far, pr)

    def fr(x, below, r):
        return below - x if r < 3 else jnp.zeros_like(x)

    def br(x, above, r):
        if r == 0:
            return x
        return x - above if r < 3 else -above

    def colsum(x):
        return jnp.sum(x, 0, keepdims=True)

    def dual_one(p, _):
        for r in range(4):
            pr = 4 * p + r
            u = natural(u0, pr, 1, 0, CP)
            below = natural(u0, pr + 1, 1, 0, CP) if r < 3 else None
            wr, wc = natural(w0, pr, 2, 0, CP), natural(w0, pr, 2, 1, CP)
            a = natural(p0, pr, 2, 0, CP) + SIGMA * (fr(u, below, r) - wr)
            b = natural(p0, pr, 2, 1, CP) + SIGMA * (fx(u, wk[0], pr) - wc)
            s = shrink(colsum(a * a + b * b), ALPHA1)
            p1r[rows_of(pr), :] = a * s
            p1c[rows_of(pr), :] = b * s
            wra = natural(w0, pr - 1, 2, 0, CP) if r > 0 else None
            wca = natural(w0, pr - 1, 2, 1, CP) if r > 0 else None
            a = natural(q0, pr, 3, 0, CP) + SIGMA * br(wr, wra, r)
            b = natural(q0, pr, 3, 1, CP) + SIGMA * bx(wc, wk[2], pr)
            c = natural(q0, pr, 3, 2, CP) + (0.5 * SIGMA) * (bx(wr, wk[1], pr) + br(wc, wca, r))
            s = shrink(colsum(a * a + b * b + 2.0 * (c * c)), ALPHA0)
            q1a[rows_of(pr), :] = a * s
            q1b[rows_of(pr), :] = b * s
            q1c[rows_of(pr), :] = c * s
        return 0

    lax.fori_loop(0, 2, dual_one, 0)

    reduce_chunk(tb, send_b, rb, fb)
    give_b = [gather(fb, gb_s, gb_r, k, me) for k in order]
    for c in give_b:
        c.start()

    def primal_one(p, _):
        for r in range(4):
            pr = 4 * p + r
            here = rows_of(pr)
            pr_, pc_ = p1r[here, :], p1c[here, :]
            above = p1r[rows_of(pr - 1), :] if r > 0 else None
            ub[here, :] = natural(u0, pr, 1, 0, CP) + TAU * (br(pr_, above, r) + bx(pc_, wk[3], pr))
            qa, qb, qc = q1a[here, :], q1b[here, :], q1c[here, :]
            qab = q1a[rows_of(pr + 1), :] if r < 3 else None
            qcb = q1c[rows_of(pr + 1), :] if r < 3 else None
            wr, wc = natural(w0, pr, 2, 0, CP), natural(w0, pr, 2, 1, CP)
            dr = TAU * (pr_ + fr(qa, qab, r) + fx(qc, wk[5], pr))
            dc = TAU * (pc_ + fx(qb, wk[4], pr) + fr(qc, qcb, r))
            nr, nc = wr + 2.0 * dr, wc + 2.0 * dc
            w1r[here, :] = wr + dr
            w1c[here, :] = wc + dc
            wbr[here, :] = nr
            wbc[here, :] = nc
            pbr[here, :] = pr_ - SIGMA * nr
            pbc[here, :] = pc_ - SIGMA * nc
        return 0

    lax.fori_loop(0, 2, primal_one, 0)

    def dual_two(p, _):
        for r in range(4):
            pr = 4 * p + r
            here = rows_of(pr)
            wr, wc = wbr[here, :], wbc[here, :]
            wra = wbr[rows_of(pr - 1), :] if r > 0 else None
            wca = wbc[rows_of(pr - 1), :] if r > 0 else None
            a = q1a[here, :] + SIGMA * br(wr, wra, r)
            b = q1b[here, :] + SIGMA * bx(wc, wk[7], pr)
            c = q1c[here, :] + (0.5 * SIGMA) * (bx(wr, wk[6], pr) + br(wc, wca, r))
            s = shrink(colsum(a * a + b * b + 2.0 * (c * c)), ALPHA0)
            q1a[here, :] = a * s
            q1b[here, :] = b * s
            q1c[here, :] = c * s
        return 0

    lax.fori_loop(0, 2, dual_two, 0)

    def aux_two(p, _):
        for r in range(4):
            pr = 4 * p + r
            here = rows_of(pr)
            qa, qb, qc = q1a[here, :], q1b[here, :], q1c[here, :]
            qab = q1a[rows_of(pr + 1), :] if r < 3 else None
            qcb = q1c[rows_of(pr + 1), :] if r < 3 else None
            v2r[here, :] = w1r[here, :] + TAU * (fr(qa, qab, r) + fx(qc, wk[9], pr))
            v2c[here, :] = w1c[here, :] + TAU * (fx(qb, wk[8], pr) + fr(qc, qcb, r))
        return 0

    lax.fori_loop(0, 2, aux_two, 0)

    take_a = [gather(fa, ga_s, ga_r, k, source(k)) for k in order]
    for c in take_a:
        c.wait_recv()

    def extrapolate(pr, acc):
        here = rows_of(pr)
        new = ub[here, :] - TAU * fa[here, :]
        bar = 2.0 * new - natural(u0, pr, 1, 0, CP)
        u1[here, :] = new
        ub1[here, :] = bar
        return pack_into(acc, bar, pr)

    own_bar = lax.fori_loop(0, NR, extrapolate, zero24)

    total = edge_c[...]
    for c, k in zip(send_e, order):
        c.wait_recv()
        total = total + edge_in[k]
    adj_w = jnp.concatenate([total, pltpu.roll(total, 127, 1), pltpu.roll(total, 126, 1)], 0)
    adj_w = jnp.where((j == 1) | (j == 6), adj_w, 0.0)
    bar_w = 2.0 * (wk[12] - TAU * adj_w) - wk[0]
    bar_w = jnp.where((j == 2) | (j == 3), own_bar, bar_w)
    a = wk[10] + SIGMA * fr_w(bar_w)
    b = wk[11] + SIGMA * fx_w(bar_w)
    s = shrink(norm_w(a * a + b * b), ALPHA1)
    wk[0] = bar_w
    wk[3] = b * s

    def dual_three(p, _):
        for r in range(4):
            pr = 4 * p + r
            here = rows_of(pr)
            u = ub1[here, :]
            below = ub1[rows_of(pr + 1), :] if r < 3 else None
            a = pbr[here, :] + SIGMA * fr(u, below, r)
            b = pbc[here, :] + SIGMA * fx(u, wk[0], pr)
            s = shrink(colsum(a * a + b * b), ALPHA1)
            a, b = a * s, b * s
            p2r[here, :] = a
            p2c[here, :] = b
            wo[pl.ds(pr, CP, stride=2 * NR), :] = v2r[here, :] + TAU * a
            wo[pl.ds(NR + pr, CP, stride=2 * NR), :] = v2c[here, :] + TAU * b
        return 0

    lax.fori_loop(0, 2, dual_three, 0)
    put_w = pltpu.make_async_copy(wo.at[pl.ds(0, NC * 2 * NR)], w_hbm, out_sem.at[1])
    put_w.start()

    take_b = [gather(fb, gb_s, gb_r, k, source(k)) for k in order]
    for c in take_b:
        c.wait_recv()
    for pr in range(NR):
        hg[pl.ds(3 * pr, 3), :] = fb[pl.ds(pr * CP + NC, CP - NC), :]
    hv = hg[...]
    gh, gl = split(jnp.concatenate([hv, pltpu.roll(hv, 64, 1)], 0)[:, 0:CP])

    def gram_step(i, _):
        bar = jnp.concatenate([ub1[rows_of(2 * i), :], ub1[rows_of(2 * i + 1), :]], 1)
        store_pair(gu, i, mm3(gh, gl, bar))
        return 0

    lax.fori_loop(0, 4, gram_step, 0)

    def primal_two(p, _):
        for r in range(4):
            pr = 4 * p + r
            here = rows_of(pr)
            m = mask[pl.ds(pr, 1), :].astype(f32) * (1.0 / (1.0 + SIGMA))
            adj = m * (fa[here, :] + SIGMA * (gu[here, :] - fb[here, :]))
            above = p2r[rows_of(pr - 1), :] if r > 0 else None
            div = br(p2r[here, :], above, r) + bx(p2c[here, :], wk[3], pr)
            uo[pl.ds(pr, CP, stride=NR), :] = u1[here, :] - TAU * (adj - div)
        return 0

    lax.fori_loop(0, 2, primal_two, 0)
    put_u = pltpu.make_async_copy(uo.at[pl.ds(0, NC * NR)], u_hbm, out_sem.at[0])
    put_u.start()

    for c in send_a + send_b + give_a + give_b + send_e + [edge_right, edge_left, halo_right, halo_left]:
        c.wait_send()
    put_w.wait()
    put_u.wait()


def body(nvox, signals, basis, response, shell_index, brain_mask, fodf, aux_field, grad_dual, sym_dual, data_dual):
    hbm = pl.BlockSpec(memory_space=pltpu.HBM)
    field = pltpu.VMEM((NR * CP, 128), f32)
    npeer = SIDE * SIDE
    dma = lambda n: pltpu.SemaphoreType.DMA((n,))
    edges = pltpu.VMEM((HALF, 128), f32)
    halos = pltpu.VMEM((8 * HALF, 128), f32)
    u, w = pl.pallas_call(
        functools.partial(kernel, nvox),
        out_shape=(
            jax.ShapeDtypeStruct((NC * NR, 128), f32),
            jax.ShapeDtypeStruct((NC * 2 * NR, 128), f32),
        ),
        in_specs=[hbm] * 10,
        out_specs=(hbm, hbm),
        scratch_shapes=[
            pltpu.VMEM((ND * NR, 128), bf16),
            pltpu.VMEM((NC, ND), f32),
            pltpu.VMEM((3, 5), f32),
            pltpu.VMEM((1, ND), jnp.int32),
            pltpu.VMEM((NR, 128), jnp.int32),
            field,
            pltpu.VMEM((CP * 2 * NR, 128), f32),
            pltpu.VMEM((CP * 2 * NR, 128), f32),
            pltpu.VMEM((CP * 3 * NR, 128), f32),
            pltpu.VMEM((ND * NR, 128), f32),
            pltpu.VMEM((ND * NR, 128), f32),
            pltpu.VMEM((CP, 128), f32),
            field, field, field, field,
            pltpu.VMEM((npeer, HALF, 128), f32),
            pltpu.VMEM((npeer, HALF, 128), f32),
            edges,
            halos, halos, halos,
            edges, edges, edges,
            pltpu.VMEM((8, 128), f32),
            pltpu.VMEM((npeer, 8, 128), f32),
            pltpu.VMEM((13, HALF, 128), f32),
        ]
        + [field] * 19
        + [
            field,
            pltpu.VMEM((CP * 2 * NR, 128), f32),
            dma(10), dma(2),
        ]
        + [dma(npeer)] * 10
        + [dma(4), dma(4)],
        compiler_params=pltpu.CompilerParams(
            collective_id=0, has_side_effects=True, vmem_limit_bytes=48 * 1024 * 1024
        ),
    )(
        signals.reshape(ND * NR, 128),
        basis.T,
        response,
        shell_index.reshape(1, ND),
        brain_mask.reshape(NR, 128),
        fodf.reshape(NC * NR, 128),
        aux_field.reshape(NC * 2 * NR, 128),
        grad_dual.reshape(NC * 2 * NR, 128),
        sym_dual.reshape(NC * 3 * NR, 128),
        data_dual.reshape(ND * NR, 128),
    )
    return u.reshape(fodf.shape), w.reshape(aux_field.shape)


def solution(mesh):
    placed = (
        P("dir", None, None, "vox"),
        P("dir", None),
        P(),
        P("dir"),
        P(None, None, "vox"),
        P(None, None, None, "vox"),
        P(None, None, None, None, "vox"),
        P(None, None, None, None, "vox"),
        P(None, None, None, None, "vox"),
        P("dir", None, None, "vox"),
    )
    return jax.shard_map(
        functools.partial(body, mesh.shape["vox"]),
        mesh=mesh,
        in_specs=placed,
        out_specs=(P(None, None, None, "vox"), P(None, None, None, None, "vox")),
        check_vma=False,
    )
```

time: 218 us -> 33.5 us (0.15)
  the two profiles are of different devices: /device:TPU:96 before, /device:TPU:6 now
where the time goes in v1:
time: 33.5 us; the launch traced here: 33.2 us
  Pallas kernels  23.9 us (71%)
  local copies, waits for them, and re-layouts  8.64 us (26%)
  between operations  0.67 us (2%)
    pallas_call x1, Pallas kernels, body(): pl.pallas_call(functools.partial(kernel, nvox), out_shape=(jax.ShapeDtype...  23.9 us
    unnamed x22, local copies, waits for them, and re-layouts  8.64 us

profile of v1, /device:TPU:6, one launch (start us, length us, event | category | flops | bytes accessed | tf_op | source)
XLA Modules:
  0.0 33.2 jit_solution(5547528656249542117)
XLA Ops:
  0.6 0.0 copy-start.7
  0.6 0.0 copy-start.8
  0.7 0.0 copy-start.9
  0.7 0.7 %copy-done.7 = s32[2,4,128]{2,1,0:T(4,128)S(1)} copy-done((s32[2,4,128]{2,1,0:T(4,128)S(1)}, s32[2,4,128]{2,1,0:T(4,128)}, u32[]{:S(2)}) %copy-start.7) | copy-done | bytes 4120
  1.3 0.0 copy-done.8
  1.3 0.0 copy-done.9
  1.3 0.0 copy-start
  1.3 1.1 %copy-done = f32[45,3,2,4,128]{4,3,2,1,0:T(4,128)S(1)} copy-done((f32[45,3,2,4,128]{4,3,2,1,0:T(4,128)S(1)}, f32[45,3,2,4,128]{4,3,2,1,0:T(4,128)}, u32[]{:S(2)}) %copy-start) | copy-done | bytes 552984
  2.4 0.0 copy-start.1
  2.4 1.0 %copy-done.1 = f32[45,2,2,4,128]{4,3,2,1,0:T(4,128)S(1)} copy-done((f32[45,2,2,4,128]{4,3,2,1,0:T(4,128)S(1)}, f32[45,2,2,4,128]{4,3,2,1,0:T(4,128)}, u32[]{:S(2)}) %copy-start.1) | copy-done | bytes 368664
  3.4 0.0 copy-start.2
  3.4 1.0 %copy-done.2 = f32[45,2,2,4,128]{4,3,2,1,0:T(4,128)S(1)} copy-done((f32[45,2,2,4,128]{4,3,2,1,0:T(4,128)S(1)}, f32[45,2,2,4,128]{4,3,2,1,0:T(4,128)}, u32[]{:S(2)}) %copy-start.2) | copy-done | bytes 368664
  4.4 0.0 copy-start.3
  4.4 1.0 %copy-done.3 = f32[72,2,4,128]{3,2,1,0:T(4,128)S(1)} copy-done((f32[72,2,4,128]{3,2,1,0:T(4,128)S(1)}, f32[72,2,4,128]{3,2,1,0:T(4,128)}, u32[]{:S(2)}) %copy-start.3) | copy-done | bytes 294936
  5.3 0.0 copy-start.4
  5.3 0.9 %copy-done.4 = f32[45,2,4,128]{3,2,1,0:T(4,128)S(1)} copy-done((f32[45,2,4,128]{3,2,1,0:T(4,128)S(1)}, f32[45,2,4,128]{3,2,1,0:T(4,128)}, u32[]{:S(2)}) %copy-start.4) | copy-done | bytes 184344
  6.2 0.0 copy-start.5
  6.3 0.9 %copy-done.5 = bf16[72,2,4,128]{3,2,1,0:T(4,128)(2,1)S(1)} copy-done((bf16[72,2,4,128]{3,2,1,0:T(4,128)(2,1)S(1)}, bf16[72,2,4,128]{3,2,1,0:T(4,128)(2,1)}, u32[]{:S(2)}) %copy-start.5) | copy-done | bytes 147480
  7.2 0.0 copy-start.6
  7.2 0.7 %copy-done.6 = f32[72,45]{0,1:T(8,128)S(1)} copy-done((f32[72,45]{0,1:T(8,128)S(1)}, f32[72,45]{0,1:T(8,128)}, u32[]{:S(2)}) %copy-start.6) | copy-done | bytes 12984
  7.9 23.9 %shard_map.113 = (f32[360,128]{1,0:T(8,128)S(1)}, f32[720,128]{1,0:T(8,128)S(1)}) custom-call(bf16[576,128]{1,0:T(8,128)(2,1)S(1)} %bitcast.18, f32[45,72]{1,0:T(8,128)S(1)} %bitcast.19, f32[3,5]{1,0:T(4,128)S(1)} %copy-done.8, s32[1,72]{1,0:T(1,128)S(1)} %bitcast.21, s32[8,128]{1,0:T(8,128)S(1)} %bitcast.20, f32[360,128]{1,0:T(8,128)S(1)} %bitcast.16, ...), custom_call_target="tpu_custom_call" | custom-call | tf_op jit(solution)/shard_map/pallas_call | solution.py:508
  31.8 0.7 %copy.14 = f32[45,2,4,128]{3,2,1,0:T(4,128)} copy(f32[45,2,4,128]{3,2,1,0:T(4,128)S(1)} %bitcast.17) | data formatting | bytes 368640
  32.4 0.7 %copy.15 = f32[45,2,2,4,128]{4,3,2,1,0:T(4,128)} copy(f32[45,2,2,4,128]{4,3,2,1,0:T(4,128)S(1)} %bitcast.14) | data formatting | bytes 737280
Async XLA Ops:
  0.6 0.7 %copy-start.7 = (s32[2,4,128]{2,1,0:T(4,128)S(1)}, s32[2,4,128]{2,1,0:T(4,128)}, u32[]{:S(2)}) copy-start(s32[2,4,128]{2,1,0:T(4,128)} %param.14) | copy-start | bytes 12292
  0.6 0.7 %copy-start.8 = (f32[3,5]{1,0:T(4,128)S(1)}, f32[3,5]{1,0:T(4,128)}, u32[]{:S(2)}) copy-start(f32[3,5]{1,0:T(4,128)} %resp_hbm.1) | copy-start | bytes 184
  0.7 0.7 %copy-start.9 = (s32[72]{0:T(128)S(1)}, s32[72]{0:T(128)}, u32[]{:S(2)}) copy-start(s32[72]{0:T(128)} %param.13) | copy-start | bytes 868
  1.3 1.1 %copy-start = (f32[45,3,2,4,128]{4,3,2,1,0:T(4,128)S(1)}, f32[45,3,2,4,128]{4,3,2,1,0:T(4,128)}, u32[]{:S(2)}) copy-start(f32[45,3,2,4,128]{4,3,2,1,0:T(4,128)} %param.18) | copy-start | bytes 1658884
  2.4 1.0 %copy-start.1 = (f32[45,2,2,4,128]{4,3,2,1,0:T(4,128)S(1)}, f32[45,2,2,4,128]{4,3,2,1,0:T(4,128)}, u32[]{:S(2)}) copy-start(f32[45,2,2,4,128]{4,3,2,1,0:T(4,128)} %param.16) | copy-start | bytes 1105924
  3.4 1.0 %copy-start.2 = (f32[45,2,2,4,128]{4,3,2,1,0:T(4,128)S(1)}, f32[45,2,2,4,128]{4,3,2,1,0:T(4,128)}, u32[]{:S(2)}) copy-start(f32[45,2,2,4,128]{4,3,2,1,0:T(4,128)} %param.17) | copy-start | bytes 1105924
  4.4 1.0 %copy-start.3 = (f32[72,2,4,128]{3,2,1,0:T(4,128)S(1)}, f32[72,2,4,128]{3,2,1,0:T(4,128)}, u32[]{:S(2)}) copy-start(f32[72,2,4,128]{3,2,1,0:T(4,128)} %param.19) | copy-start | bytes 884740
  5.3 0.9 %copy-start.4 = (f32[45,2,4,128]{3,2,1,0:T(4,128)S(1)}, f32[45,2,4,128]{3,2,1,0:T(4,128)}, u32[]{:S(2)}) copy-start(f32[45,2,4,128]{3,2,1,0:T(4,128)} %param.15) | copy-start | bytes 552964
  6.2 0.9 %copy-start.5 = (bf16[72,2,4,128]{3,2,1,0:T(4,128)(2,1)S(1)}, bf16[72,2,4,128]{3,2,1,0:T(4,128)(2,1)}, u32[]{:S(2)}) copy-start(bf16[72,2,4,128]{3,2,1,0:T(4,128)(2,1)} %param.10) | copy-start | bytes 442372
  7.2 0.7 %copy-start.6 = (f32[72,45]{0,1:T(8,128)S(1)}, f32[72,45]{0,1:T(8,128)}, u32[]{:S(2)}) copy-start(f32[72,45]{0,1:T(8,128)} %param.11) | copy-start | bytes 38884

commit v2 on v1

--- a/solution.py
+++ b/solution.py
@@ -48,13 +48,12 @@
 def kernel(
     nvox,
     sig_hbm, basis_hbm, resp_hbm, shell_hbm, mask_hbm, fodf_hbm, aux_hbm, grad_hbm, sym_hbm, dual_hbm,
-    u_hbm, w_hbm,
+    uo, wo,
     sig, basis, resp, shell, mask, u0, w0, p0, q0, y0, sigf,
     kt, ta, tb, fa, fb, ra, rb, hg,
     halo, halo_l, halo_r, edge, edge_l, edge_r, edge_c, edge_in, wk,
     p1r, p1c, q1a, q1b, q1c, wbr, wbc, w1r, w1c, pbr, pbc, ub, v2r, v2c, u1, ub1, gu, p2r, p2c,
-    uo, wo,
-    in_sem, out_sem, sa_s, sa_r, sb_s, sb_r, ga_s, ga_r, gb_s, gb_r, ec_s, ec_r, vox_s, vox_r,
+    in_sem, sa_s, sa_r, sb_s, sb_r, ga_s, ga_r, gb_s, gb_r, ec_s, ec_r, vox_s, vox_r,
 ):
     me = lax.axis_index("dir")
     vox = lax.axis_index("vox")
@@ -459,8 +458,6 @@
         return 0
 
     lax.fori_loop(0, 2, dual_three, 0)
-    put_w = pltpu.make_async_copy(wo.at[pl.ds(0, NC * 2 * NR)], w_hbm, out_sem.at[1])
-    put_w.start()
 
     take_b = [gather(fb, gb_s, gb_r, k, source(k)) for k in order]
     for c in take_b:
@@ -489,17 +486,25 @@
         return 0
 
     lax.fori_loop(0, 2, primal_two, 0)
-    put_u = pltpu.make_async_copy(uo.at[pl.ds(0, NC * NR)], u_hbm, out_sem.at[0])
-    put_u.start()
 
     for c in send_a + send_b + give_a + give_b + send_e + [edge_right, edge_left, halo_right, halo_left]:
         c.wait_send()
-    put_w.wait()
-    put_u.wait()
+
+
+def put_kernel(u, w, u_hbm, w_hbm, sem):
+    copies = [
+        pltpu.make_async_copy(w.at[pl.ds(0, NC * 2 * NR)], w_hbm, sem.at[0]),
+        pltpu.make_async_copy(u.at[pl.ds(0, NC * NR)], u_hbm, sem.at[1]),
+    ]
+    for c in copies:
+        c.start()
+    for c in copies:
+        c.wait()
 
 
 def body(nvox, signals, basis, response, shell_index, brain_mask, fodf, aux_field, grad_dual, sym_dual, data_dual):
     hbm = pl.BlockSpec(memory_space=pltpu.HBM)
+    vmem = pl.BlockSpec(memory_space=pltpu.VMEM)
     field = pltpu.VMEM((NR * CP, 128), f32)
     npeer = SIDE * SIDE
     dma = lambda n: pltpu.SemaphoreType.DMA((n,))
@@ -507,12 +512,9 @@
     halos = pltpu.VMEM((8 * HALF, 128), f32)
     u, w = pl.pallas_call(
         functools.partial(kernel, nvox),
-        out_shape=(
-            jax.ShapeDtypeStruct((NC * NR, 128), f32),
-            jax.ShapeDtypeStruct((NC * 2 * NR, 128), f32),
-        ),
+        out_shape=(pltpu.VMEM((NR * CP, 128), f32), pltpu.VMEM((CP * 2 * NR, 128), f32)),
         in_specs=[hbm] * 10,
-        out_specs=(hbm, hbm),
+        out_specs=(vmem, vmem),
         scratch_shapes=[
             pltpu.VMEM((ND * NR, 128), bf16),
             pltpu.VMEM((NC, ND), f32),
@@ -537,17 +539,13 @@
             pltpu.VMEM((13, HALF, 128), f32),
         ]
         + [field] * 19
-        + [
-            field,
-            pltpu.VMEM((CP * 2 * NR, 128), f32),
-            dma(10), dma(2),
-        ]
+        + [dma(10)]
         + [dma(npeer)] * 10
         + [dma(4), dma(4)],
         compiler_params=pltpu.CompilerParams(
             collective_id=0, has_side_effects=True, vmem_limit_bytes=48 * 1024 * 1024
         ),
-    )(
+    )(*[pltpu.with_memory_space_constraint(x, pltpu.HBM) for x in (
         signals.reshape(ND * NR, 128),
         basis.T,
         response,
@@ -558,7 +556,15 @@
         grad_dual.reshape(NC * 2 * NR, 128),
         sym_dual.reshape(NC * 3 * NR, 128),
         data_dual.reshape(ND * NR, 128),
-    )
+    )])
+    u, w = pl.pallas_call(
+        put_kernel,
+        out_shape=(pltpu.HBM((NC * NR, 128), f32), pltpu.HBM((NC * 2 * NR, 128), f32)),
+        in_specs=[vmem, vmem],
+        out_specs=(hbm, hbm),
+        scratch_shapes=[dma(2)],
+        compiler_params=pltpu.CompilerParams(vmem_limit_bytes=4 * 1024 * 1024),
+    )(pltpu.with_memory_space_constraint(u, pltpu.VMEM), pltpu.with_memory_space_constraint(w, pltpu.VMEM))
     return u.reshape(fodf.shape), w.reshape(aux_field.shape)
 
 

time: 33.5 us -> 24.8 us (0.74)
  the two profiles are of different devices: /device:TPU:6 before, /device:TPU:8 now
where the time goes in v2:
time: 24.8 us; the launch traced here: 24.7 us
  Pallas kernels  24 us (97%)
  between operations  0.64 us (3%)
    pallas_call x1, Pallas kernels, body(): pl.pallas_call(functools.partial(kernel, nvox), out_shape=(pltpu.VMEM((NR...  23.2 us
    pallas_call x1, Pallas kernels, body(): pl.pallas_call(put_kernel, out_shape=(pltpu.HBM((NC * NR, 128), f32), plt...  0.81 us

profile of v2, /device:TPU:8, one launch (start us, length us, event | category | flops | bytes accessed | tf_op | source)
XLA Modules:
  0.0 24.7 jit_solution(250454392390942332)
XLA Ops:
  0.6 23.2 %shard_map.113 = (f32[384,128]{1,0:T(8,128)S(1)}, f32[768,128]{1,0:T(8,128)S(1)}) custom-call(bf16[576,128]{1,0:T(8,128)(2,1)} %bitcast.16, f32[45,72]{1,0:T(8,128)} %bitcast.17, f32[3,5]{1,0:T(4,128)} %resp_hbm.1, s32[1,72]{1,0:T(1,128)} %bitcast.19, s32[8,128]{1,0:T(8,128)} %bitcast.18, f32[360,128]{1,0:T(8,128)} %bitcast.15, f32[720,128]{1,0:T(8,128)} %bitcast.12, ...), custom_call_target="tpu_custom_call" | custom-call | tf_op jit(solution)/shard_map/pallas_call | solution.py:513
  23.9 0.8 %shard_map.114 = (f32[360,128]{1,0:T(8,128)}, f32[720,128]{1,0:T(8,128)}) custom-call(f32[384,128]{1,0:T(8,128)S(1)} %get-tuple-element.6.u, f32[768,128]{1,0:T(8,128)S(1)} %get-tuple-element.7.w), custom_call_target="tpu_custom_call" | custom-call | tf_op jit(solution)/shard_map/pallas_call | solution.py:560

commit v3 on v2

--- a/solution.py
+++ b/solution.py
@@ -52,8 +52,8 @@
     sig, basis, resp, shell, mask, u0, w0, p0, q0, y0, sigf,
     kt, ta, tb, fa, fb, ra, rb, hg,
     halo, halo_l, halo_r, edge, edge_l, edge_r, edge_c, edge_in, wk,
-    p1r, p1c, q1a, q1b, q1c, wbr, wbc, w1r, w1c, pbr, pbc, ub, v2r, v2c, u1, ub1, gu, p2r, p2c,
-    in_sem, sa_s, sa_r, sb_s, sb_r, ga_s, ga_r, gb_s, gb_r, ec_s, ec_r, vox_s, vox_r,
+    p1r, p1c, q1a, q1b, q1c, wbr, wbc, w1r, w1c, pbr, pbc, ub, v2r, v2c, u1, gu, p2r, p2c,
+    in_sem, dir_s, dir_r, vox_s, vox_r,
 ):
     me = lax.axis_index("dir")
     vox = lax.axis_index("vox")
@@ -64,10 +64,8 @@
     def peer(k):
         return lax.rem(mx + k // SIDE, SIDE) * SIDE + lax.rem(my + k % SIDE, SIDE)
 
-    def source(k):
-        return lax.rem(mx + SIDE - k // SIDE, SIDE) * SIDE + lax.rem(my + SIDE - k % SIDE, SIDE)
-
-    right, left = lax.rem(vox + 1, nvox), lax.rem(vox + nvox - 1, nvox)
+    has_left, has_right = vox > 0, vox < nvox - 1
+    left, right = vox - 1, vox + 1
 
     def load(i, src, dst):
         return pltpu.make_async_copy(src, dst, in_sem.at[i])
@@ -84,14 +82,17 @@
         load(8, grad_hbm, p0.at[pl.ds(0, NC * 2 * NR)]),
         load(9, sym_hbm, q0.at[pl.ds(0, NC * 3 * NR)]),
     ]
-    for c in loads:
-        c.start()
-
     barrier = pltpu.get_barrier_semaphore()
     for k in order:
         pl.semaphore_signal(barrier, inc=1, device_id={"dir": peer(k)}, device_id_type=MESH)
-    for n in (left, right):
-        pl.semaphore_signal(barrier, inc=1, device_id={"vox": n}, device_id_type=MESH)
+    for there, n in ((has_left, left), (has_right, right)):
+
+        @pl.when(there)
+        def _():
+            pl.semaphore_signal(barrier, inc=1, device_id={"vox": n}, device_id_type=MESH)
+
+    for c in loads[:7]:
+        c.start()
 
     lane = lax.broadcasted_iota(jnp.int32, (1, 128), 1)
     for ref, n in ((u0, 1), (w0, 2), (p0, 2), (q0, 3)):
@@ -116,6 +117,10 @@
     knh128, knl128 = split(knv)
     knh, knl = knh128[:, 0:CP], knl128[:, 0:CP]
 
+    for c in loads[7:]:
+        c.start()
+    gram = mm3(kth, ktl, knv)
+    hg[...] = gram[0:HALF] + pltpu.roll(gram[HALF:CP], 64, 1)
     for c in loads[3:7]:
         c.wait()
 
@@ -143,29 +148,61 @@
         store_pair(ta, i, mm3(kth, ktl, y))
         return 0
 
-    lax.fori_loop(0, 4, data_step, 0)
+    lax.fori_loop(0, 4, data_step, 0, unroll=True)
+
+    for pr in range(NR):
+        ta[pl.ds(pr * CP + NC, CP - NC), :] = hg[pl.ds(3 * pr, 3), :]
 
     def chunk(d):
         return pl.ds(pl.multiple_of(d * HALF, HALF), HALF)
 
-    def scatter(src, dst, ss, rs, k):
-        return pltpu.make_async_remote_copy(
-            src_ref=src.at[chunk(peer(k))], dst_ref=dst.at[k], send_sem=ss.at[k], recv_sem=rs.at[k],
-            device_id={"dir": peer(k)}, device_id_type=MESH)
-
-    def gather(ref, ss, rs, k, at):
-        return pltpu.make_async_remote_copy(
-            src_ref=ref.at[chunk(at)], dst_ref=ref.at[chunk(at)], send_sem=ss.at[k], recv_sem=rs.at[k],
-            device_id={"dir": peer(k)}, device_id_type=MESH)
+    def scatter(src, dst, n):
+        return [
+            pltpu.make_async_remote_copy(
+                src_ref=src.at[chunk(peer(k))], dst_ref=dst.at[i], send_sem=dir_s.at[n], recv_sem=dir_r.at[n],
+                device_id={"dir": peer(k)}, device_id_type=MESH)
+            for i, k in enumerate(order)
+        ]
+
+    def gather(ref, n):
+        return [
+            pltpu.make_async_remote_copy(
+                src_ref=ref.at[chunk(me)], dst_ref=ref.at[chunk(me)], send_sem=dir_s.at[n], recv_sem=dir_r.at[n],
+                device_id={"dir": peer(k)}, device_id_type=MESH)
+            for k in order
+        ]
+
+    def wait_all(sem, ref):
+        pltpu.make_async_copy(ref, ref, sem).wait()
 
     def to_vox(src, dst, n, k):
         return pltpu.make_async_remote_copy(
             src_ref=src, dst_ref=dst, send_sem=vox_s.at[k], recv_sem=vox_r.at[k],
             device_id={"vox": n}, device_id_type=MESH)
 
-    pl.semaphore_wait(barrier, npeer - 1 + 2)
-    send_a = [scatter(ta, ra, sa_s, sa_r, k) for k in order]
-    for c in send_a:
+    def start_vox(to_right, to_left):
+        @pl.when(has_right)
+        def _():
+            to_right.start()
+
+        @pl.when(has_left)
+        def _():
+            to_left.start()
+
+    def arrive_vox(to_right, to_left):
+        @pl.when(has_left)
+        def _():
+            to_right.wait_recv()
+
+        @pl.when(has_right)
+        def _():
+            to_left.wait_recv()
+
+    others = npeer - 1
+    slots = pl.ds(0, others)
+    rows_in = pl.ds(0, others * HALF)
+    pl.semaphore_wait(barrier, others + has_left.astype(jnp.int32) + has_right.astype(jnp.int32))
+    for c in scatter(ta, ra, 0):
         c.start()
 
     slot_of = lane // 8
@@ -180,9 +217,8 @@
 
     zero24 = jnp.zeros((HALF, 128), f32)
     edge[...] = lax.fori_loop(0, NR, lambda pr, acc: pack_into(acc, ta[rows_of(pr), :], pr), zero24)
-    edge_right, edge_left = to_vox(edge, edge_l, right, 0), to_vox(edge, edge_r, left, 1)
-    edge_right.start()
-    edge_left.start()
+    edges = to_vox(edge, edge_l, right, 0), to_vox(edge, edge_r, left, 1)
+    start_vox(*edges)
 
     def signal_step(i, _):
         s = pair(sigf, i, ND).astype(bf16)
@@ -190,12 +226,7 @@
         return 0
 
     lax.fori_loop(0, 4, signal_step, 0)
-    gram = mm3(kth, ktl, knv)
-    hpart = gram[0:HALF] + pltpu.roll(gram[HALF:CP], 64, 1)
-    for pr in range(NR):
-        tb[pl.ds(pr * CP + NC, CP - NC), :] = hpart[3 * pr : 3 * pr + 3]
-    send_b = [scatter(tb, rb, sb_s, sb_r, k) for k in order]
-    for c in send_b:
+    for c in scatter(tb, rb, 1):
         c.start()
 
     for c in loads[7:]:
@@ -209,40 +240,34 @@
     packed = lax.fori_loop(0, NR, pack_step, (zero24,) * 8)
     for f in range(8):
         halo[pl.ds(f * HALF, HALF), :] = packed[f]
-    halo_right, halo_left = to_vox(halo, halo_l, right, 2), to_vox(halo, halo_r, left, 3)
-    halo_right.start()
-    halo_left.start()
-
-    def reduce_chunk(src, scattered, recv, full):
+    halos = to_vox(halo, halo_l, right, 2), to_vox(halo, halo_r, left, 3)
+    start_vox(*halos)
+
+    arrive_vox(*edges)
+    near = (
+        jnp.where((j == 1) & has_left, edge_l[...], 0.0)
+        + jnp.where(j == 2, edge[...], 0.0)
+        + jnp.where((j == 6) & has_right, pltpu.roll(edge_r[...], 4, 1), 0.0)
+    )
+    edge_c[pl.ds(0, 8), :] = near[0:8] + pltpu.roll(near[8:16], 2, 1)
+    edge_c[pl.ds(8, 8), :] = near[16:24]
+    for i, k in enumerate(order):
+        pltpu.make_async_remote_copy(
+            src_ref=edge_c, dst_ref=edge_in.at[i], send_sem=dir_s.at[4], recv_sem=dir_r.at[4],
+            device_id={"dir": peer(k)}, device_id_type=MESH).start()
+
+    def reduce_chunk(src, recv, n, full):
+        wait_all(dir_r.at[n], recv.at[slots])
         total = src[chunk(me), :]
-        for c, k in zip(scattered, order):
-            c.wait_recv()
-            total = total + recv[k]
+        for i in range(others):
+            total = total + recv[i]
         full[chunk(me), :] = total
-
-    reduce_chunk(ta, send_a, ra, fa)
-    give_a = [gather(fa, ga_s, ga_r, k, me) for k in order]
-    for c in give_a:
-        c.start()
-
-    has_left = vox > 0
-    has_right = vox < nvox - 1
-    edge_right.wait_recv()
-    edge_left.wait_recv()
-    near = jnp.where((j == 1) & has_left, edge_l[...], 0.0) + jnp.where((j == 6) & has_right, pltpu.roll(edge_r[...], 4, 1), 0.0)
-    edge_c[...] = near[0:8] + pltpu.roll(near[8:16], 1, 1) + pltpu.roll(near[16:24], 2, 1)
-
-    def spread(k):
-        return pltpu.make_async_remote_copy(
-            src_ref=edge_c, dst_ref=edge_in.at[k], send_sem=ec_s.at[k], recv_sem=ec_r.at[k],
-            device_id={"dir": peer(k)}, device_id_type=MESH)
-
-    send_e = [spread(k) for k in order]
-    for c in send_e:
-        c.start()
-
-    halo_right.wait_recv()
-    halo_left.wait_recv()
+        for c in gather(full, n + 2):
+            c.start()
+
+    reduce_chunk(ta, ra, 0, fa)
+
+    arrive_vox(*halos)
 
     def widen(f):
         at = pl.ds(f * HALF, HALF)
@@ -299,6 +324,8 @@
     ubw = uw + TAU * (br_w(p1rw) + bx_w(p1cw))
     for n, val in enumerate((uw, wrw, wcw, p1cw, q1bw, q1cw, wbrw, wbcw, q2bw, q2cw, pbrw, pbcw, ubw)):
         wk[n] = val
+
+    reduce_chunk(tb, rb, 1, fb)
 
     keep = jnp.where(lane + vox * 128 < nvox * 128 - 1, 1.0, 0.0).astype(f32)
 
@@ -353,10 +380,6 @@
 
     lax.fori_loop(0, 2, dual_one, 0)
 
-    reduce_chunk(tb, send_b, rb, fb)
-    give_b = [gather(fb, gb_s, gb_r, k, me) for k in order]
-    for c in give_b:
-        c.start()
 
     def primal_one(p, _):
         for r in range(4):
@@ -413,42 +436,42 @@
 
     lax.fori_loop(0, 2, aux_two, 0)
 
-    take_a = [gather(fa, ga_s, ga_r, k, source(k)) for k in order]
-    for c in take_a:
-        c.wait_recv()
-
-    def extrapolate(pr, acc):
-        here = rows_of(pr)
-        new = ub[here, :] - TAU * fa[here, :]
-        bar = 2.0 * new - natural(u0, pr, 1, 0, CP)
-        u1[here, :] = new
-        ub1[here, :] = bar
-        return pack_into(acc, bar, pr)
-
-    own_bar = lax.fori_loop(0, NR, extrapolate, zero24)
-
+    wait_all(dir_r.at[4], edge_in.at[slots])
     total = edge_c[...]
-    for c, k in zip(send_e, order):
-        c.wait_recv()
-        total = total + edge_in[k]
-    adj_w = jnp.concatenate([total, pltpu.roll(total, 127, 1), pltpu.roll(total, 126, 1)], 0)
-    adj_w = jnp.where((j == 1) | (j == 6), adj_w, 0.0)
+    for i in range(others):
+        total = total + edge_in[i]
+    adj_w = jnp.concatenate([total[0:8], pltpu.roll(total[0:8], 126, 1), total[8:16]], 0)
+    row24 = lax.broadcasted_iota(jnp.int32, (HALF, 1), 0)
+    adj_w = jnp.where(((j == 1) | (j == 2) | (j == 6)) & ((row24 < NC - HALF) | (lane < 64)), adj_w, 0.0)
     bar_w = 2.0 * (wk[12] - TAU * adj_w) - wk[0]
-    bar_w = jnp.where((j == 2) | (j == 3), own_bar, bar_w)
     a = wk[10] + SIGMA * fr_w(bar_w)
     b = wk[11] + SIGMA * fx_w(bar_w)
     s = shrink(norm_w(a * a + b * b), ALPHA1)
     wk[0] = bar_w
     wk[3] = b * s
 
+    wait_all(dir_r.at[2], fa.at[rows_in])
+    for pr in range(NR):
+        hg[pl.ds(3 * pr, 3), :] = fa[pl.ds(pr * CP + NC, CP - NC), :]
+    hv = hg[...]
+    gh, gl = split(jnp.concatenate([hv, pltpu.roll(hv, 64, 1)], 0)[:, 0:CP])
+    real = lax.broadcasted_iota(jnp.int32, (CP, 1), 0) < NC
+
     def dual_three(p, _):
+        bars = []
         for r in range(4):
             pr = 4 * p + r
             here = rows_of(pr)
-            u = ub1[here, :]
-            below = ub1[rows_of(pr + 1), :] if r < 3 else None
-            a = pbr[here, :] + SIGMA * fr(u, below, r)
-            b = pbc[here, :] + SIGMA * fx(u, wk[0], pr)
+            new = ub[here, :] - TAU * jnp.where(real, fa[here, :], 0.0)
+            u1[here, :] = new
+            bars.append(2.0 * new - natural(u0, pr, 1, 0, CP))
+        for i in range(2):
+            store_pair(gu, 2 * p + i, mm3(gh, gl, jnp.concatenate(bars[2 * i : 2 * i + 2], 1)))
+        for r in range(4):
+            pr = 4 * p + r
+            here = rows_of(pr)
+            a = pbr[here, :] + SIGMA * fr(bars[r], bars[r + 1] if r < 3 else None, r)
+            b = pbc[here, :] + SIGMA * fx(bars[r], wk[0], pr)
             s = shrink(colsum(a * a + b * b), ALPHA1)
             a, b = a * s, b * s
             p2r[here, :] = a
@@ -458,21 +481,7 @@
         return 0
 
     lax.fori_loop(0, 2, dual_three, 0)
-
-    take_b = [gather(fb, gb_s, gb_r, k, source(k)) for k in order]
-    for c in take_b:
-        c.wait_recv()
-    for pr in range(NR):
-        hg[pl.ds(3 * pr, 3), :] = fb[pl.ds(pr * CP + NC, CP - NC), :]
-    hv = hg[...]
-    gh, gl = split(jnp.concatenate([hv, pltpu.roll(hv, 64, 1)], 0)[:, 0:CP])
-
-    def gram_step(i, _):
-        bar = jnp.concatenate([ub1[rows_of(2 * i), :], ub1[rows_of(2 * i + 1), :]], 1)
-        store_pair(gu, i, mm3(gh, gl, bar))
-        return 0
-
-    lax.fori_loop(0, 4, gram_step, 0)
+    wait_all(dir_r.at[3], fb.at[rows_in])
 
     def primal_two(p, _):
         for r in range(4):
@@ -487,8 +496,20 @@
 
     lax.fori_loop(0, 2, primal_two, 0)
 
-    for c in send_a + send_b + give_a + give_b + send_e + [edge_right, edge_left, halo_right, halo_left]:
-        c.wait_send()
+    wait_all(dir_s.at[0], ra.at[slots])
+    wait_all(dir_s.at[1], rb.at[slots])
+    wait_all(dir_s.at[2], fa.at[rows_in])
+    wait_all(dir_s.at[3], fb.at[rows_in])
+    wait_all(dir_s.at[4], edge_in.at[slots])
+    for to_right, to_left in (edges, halos):
+
+        @pl.when(has_right)
+        def _():
+            to_right.wait_send()
+
+        @pl.when(has_left)
+        def _():
+            to_left.wait_send()
 
 
 def put_kernel(u, w, u_hbm, w_hbm, sem):
@@ -534,14 +555,13 @@
             edges,
             halos, halos, halos,
             edges, edges, edges,
-            pltpu.VMEM((8, 128), f32),
-            pltpu.VMEM((npeer, 8, 128), f32),
+            pltpu.VMEM((16, 128), f32),
+            pltpu.VMEM((npeer, 16, 128), f32),
             pltpu.VMEM((13, HALF, 128), f32),
         ]
-        + [field] * 19
+        + [field] * 18
         + [dma(10)]
-        + [dma(npeer)] * 10
-        + [dma(4), dma(4)],
+        + [dma(5), dma(5), dma(4), dma(4)],
         compiler_params=pltpu.CompilerParams(
             collective_id=0, has_side_effects=True, vmem_limit_bytes=48 * 1024 * 1024
         ),

time: 24.8 us -> 20.9 us (0.84)
  the two profiles are of different devices: /device:TPU:8 before, /device:TPU:96 now
where the time goes in v3:
time: 20.9 us; the launch traced here: 20.8 us
  Pallas kernels  20.1 us (96%)
  between operations  0.64 us (3%)
    pallas_call x1, Pallas kernels, body(): pl.pallas_call(functools.partial(kernel, nvox), out_shape=(pltpu.VMEM((NR...  19.3 us
    pallas_call x1, Pallas kernels, body(): pl.pallas_call(put_kernel, out_shape=(pltpu.HBM((NC * NR, 128), f32), plt...  0.81 us

profile of v3, /device:TPU:96, one launch (start us, length us, event | category | flops | bytes accessed | tf_op | source)
XLA Modules:
  0.0 20.8 jit_solution(6250515040516143064)
XLA Ops:
  0.6 19.3 %shard_map.113 = (f32[384,128]{1,0:T(8,128)S(1)}, f32[768,128]{1,0:T(8,128)S(1)}) custom-call(bf16[576,128]{1,0:T(8,128)(2,1)} %bitcast.16, f32[45,72]{1,0:T(8,128)} %bitcast.17, f32[3,5]{1,0:T(4,128)} %resp_hbm.1, s32[1,72]{1,0:T(1,128)} %bitcast.19, s32[8,128]{1,0:T(8,128)} %bitcast.18, f32[360,128]{1,0:T(8,128)} %bitcast.15, f32[720,128]{1,0:T(8,128)} %bitcast.12, ...), custom_call_target="tpu_custom_call" | custom-call | tf_op jit(solution)/shard_map/pallas_call | solution.py:534
  19.9 0.8 %shard_map.114 = (f32[360,128]{1,0:T(8,128)}, f32[720,128]{1,0:T(8,128)}) custom-call(f32[384,128]{1,0:T(8,128)S(1)} %get-tuple-element.6.u, f32[768,128]{1,0:T(8,128)S(1)} %get-tuple-element.7.w), custom_call_target="tpu_custom_call" | custom-call | tf_op jit(solution)/shard_map/pallas_call | solution.py:580

commit v4 on v3

--- a/solution.py
+++ b/solution.py
@@ -82,6 +82,8 @@
         load(8, grad_hbm, p0.at[pl.ds(0, NC * 2 * NR)]),
         load(9, sym_hbm, q0.at[pl.ds(0, NC * 3 * NR)]),
     ]
+    for c in loads[:7]:
+        c.start()
     barrier = pltpu.get_barrier_semaphore()
     for k in order:
         pl.semaphore_signal(barrier, inc=1, device_id={"dir": peer(k)}, device_id_type=MESH)
@@ -91,8 +93,6 @@
         def _():
             pl.semaphore_signal(barrier, inc=1, device_id={"vox": n}, device_id_type=MESH)
 
-    for c in loads[:7]:
-        c.start()
 
     lane = lax.broadcasted_iota(jnp.int32, (1, 128), 1)
     for ref, n in ((u0, 1), (w0, 2), (p0, 2), (q0, 3)):
@@ -153,6 +153,12 @@
     for pr in range(NR):
         ta[pl.ds(pr * CP + NC, CP - NC), :] = hg[pl.ds(3 * pr, 3), :]
 
+    def signal_step(i, _):
+        s = pair(sigf, i, ND).astype(bf16)
+        store_pair(tb, i, mm(kth, s) + mm(ktl, s))
+        return 0
+
+    lax.fori_loop(0, 4, signal_step, 0, unroll=True)
     def chunk(d):
         return pl.ds(pl.multiple_of(d * HALF, HALF), HALF)
 
@@ -202,8 +208,12 @@
     slots = pl.ds(0, others)
     rows_in = pl.ds(0, others * HALF)
     pl.semaphore_wait(barrier, others + has_left.astype(jnp.int32) + has_right.astype(jnp.int32))
-    for c in scatter(ta, ra, 0):
-        c.start()
+    far = [min(k // SIDE, SIDE - k // SIDE) + min(k % SIDE, SIDE - k % SIDE) for k in order]
+    sends = scatter(ta, ra, 0), scatter(tb, rb, 1)
+    for n, least, most in ((0, 2, 4), (1, 3, 4), (0, 1, 1), (1, 2, 2), (1, 1, 1)):
+        for c, hops in zip(sends[n], far):
+            if least <= hops <= most:
+                c.start()
 
     slot_of = lane // 8
     j = lax.rem(lane, 8)
@@ -220,15 +230,6 @@
     edges = to_vox(edge, edge_l, right, 0), to_vox(edge, edge_r, left, 1)
     start_vox(*edges)
 
-    def signal_step(i, _):
-        s = pair(sigf, i, ND).astype(bf16)
-        store_pair(tb, i, mm(kth, s) + mm(ktl, s))
-        return 0
-
-    lax.fori_loop(0, 4, signal_step, 0)
-    for c in scatter(tb, rb, 1):
-        c.start()
-
     for c in loads[7:]:
         c.wait()
 
@@ -246,11 +247,9 @@
     arrive_vox(*edges)
     near = (
         jnp.where((j == 1) & has_left, edge_l[...], 0.0)
-        + jnp.where(j == 2, edge[...], 0.0)
         + jnp.where((j == 6) & has_right, pltpu.roll(edge_r[...], 4, 1), 0.0)
     )
-    edge_c[pl.ds(0, 8), :] = near[0:8] + pltpu.roll(near[8:16], 2, 1)
-    edge_c[pl.ds(8, 8), :] = near[16:24]
+    edge_c[...] = near[0:8] + pltpu.roll(near[8:16], 1, 1) + pltpu.roll(near[16:24], 2, 1)
     for i, k in enumerate(order):
         pltpu.make_async_remote_copy(
             src_ref=edge_c, dst_ref=edge_in.at[i], send_sem=dir_s.at[4], recv_sem=dir_r.at[4],
@@ -266,6 +265,7 @@
             c.start()
 
     reduce_chunk(ta, ra, 0, fa)
+    reduce_chunk(tb, rb, 1, fb)
 
     arrive_vox(*halos)
 
@@ -324,8 +324,6 @@
     ubw = uw + TAU * (br_w(p1rw) + bx_w(p1cw))
     for n, val in enumerate((uw, wrw, wcw, p1cw, q1bw, q1cw, wbrw, wbcw, q2bw, q2cw, pbrw, pbcw, ubw)):
         wk[n] = val
-
-    reduce_chunk(tb, rb, 1, fb)
 
     keep = jnp.where(lane + vox * 128 < nvox * 128 - 1, 1.0, 0.0).astype(f32)
 
@@ -440,15 +438,11 @@
     total = edge_c[...]
     for i in range(others):
         total = total + edge_in[i]
-    adj_w = jnp.concatenate([total[0:8], pltpu.roll(total[0:8], 126, 1), total[8:16]], 0)
+    adj_w = jnp.concatenate([total, pltpu.roll(total, 127, 1), pltpu.roll(total, 126, 1)], 0)
     row24 = lax.broadcasted_iota(jnp.int32, (HALF, 1), 0)
-    adj_w = jnp.where(((j == 1) | (j == 2) | (j == 6)) & ((row24 < NC - HALF) | (lane < 64)), adj_w, 0.0)
+    adj_w = jnp.where(((j == 1) | (j == 6)) & ((row24 < NC - HALF) | (lane < 64)), adj_w, 0.0)
     bar_w = 2.0 * (wk[12] - TAU * adj_w) - wk[0]
-    a = wk[10] + SIGMA * fr_w(bar_w)
-    b = wk[11] + SIGMA * fx_w(bar_w)
-    s = shrink(norm_w(a * a + b * b), ALPHA1)
     wk[0] = bar_w
-    wk[3] = b * s
 
     wait_all(dir_r.at[2], fa.at[rows_in])
     for pr in range(NR):
@@ -457,7 +451,7 @@
     gh, gl = split(jnp.concatenate([hv, pltpu.roll(hv, 64, 1)], 0)[:, 0:CP])
     real = lax.broadcasted_iota(jnp.int32, (CP, 1), 0) < NC
 
-    def dual_three(p, _):
+    def dual_three(p, own_bar):
         bars = []
         for r in range(4):
             pr = 4 * p + r
@@ -465,6 +459,7 @@
             new = ub[here, :] - TAU * jnp.where(real, fa[here, :], 0.0)
             u1[here, :] = new
             bars.append(2.0 * new - natural(u0, pr, 1, 0, CP))
+            own_bar = pack_into(own_bar, bars[r], pr)
         for i in range(2):
             store_pair(gu, 2 * p + i, mm3(gh, gl, jnp.concatenate(bars[2 * i : 2 * i + 2], 1)))
         for r in range(4):
@@ -478,23 +473,34 @@
             p2c[here, :] = b
             wo[pl.ds(pr, CP, stride=2 * NR), :] = v2r[here, :] + TAU * a
             wo[pl.ds(NR + pr, CP, stride=2 * NR), :] = v2c[here, :] + TAU * b
-        return 0
-
-    lax.fori_loop(0, 2, dual_three, 0)
-    wait_all(dir_r.at[3], fb.at[rows_in])
-
+        return own_bar
+
+    own_bar = lax.fori_loop(0, 2, dual_three, zero24)
+    bar_w = jnp.where(j == 2, own_bar, wk[0])
+    a = wk[10] + SIGMA * fr_w(bar_w)
+    b = wk[11] + SIGMA * fx_w(bar_w)
+    s = shrink(norm_w(a * a + b * b), ALPHA1)
+    wk[3] = b * s
     def primal_two(p, _):
         for r in range(4):
             pr = 4 * p + r
             here = rows_of(pr)
             m = mask[pl.ds(pr, 1), :].astype(f32) * (1.0 / (1.0 + SIGMA))
-            adj = m * (fa[here, :] + SIGMA * (gu[here, :] - fb[here, :]))
             above = p2r[rows_of(pr - 1), :] if r > 0 else None
             div = br(p2r[here, :], above, r) + bx(p2c[here, :], wk[3], pr)
-            uo[pl.ds(pr, CP, stride=NR), :] = u1[here, :] - TAU * (adj - div)
+            adj = m * (fa[here, :] + SIGMA * gu[here, :])
+            u1[here, :] = u1[here, :] - TAU * (adj - div)
         return 0
 
     lax.fori_loop(0, 2, primal_two, 0)
+    wait_all(dir_r.at[3], fb.at[rows_in])
+
+    def add_signals(pr, _):
+        m = mask[pl.ds(pr, 1), :].astype(f32) * (TAU * SIGMA / (1.0 + SIGMA))
+        uo[pl.ds(pr, CP, stride=NR), :] = u1[rows_of(pr), :] + m * fb[rows_of(pr), :]
+        return 0
+
+    lax.fori_loop(0, NR, add_signals, 0, unroll=True)
 
     wait_all(dir_s.at[0], ra.at[slots])
     wait_all(dir_s.at[1], rb.at[slots])
@@ -555,8 +561,8 @@
             edges,
             halos, halos, halos,
             edges, edges, edges,
-            pltpu.VMEM((16, 128), f32),
-            pltpu.VMEM((npeer, 16, 128), f32),
+            pltpu.VMEM((8, 128), f32),
+            pltpu.VMEM((npeer, 8, 128), f32),
             pltpu.VMEM((13, HALF, 128), f32),
         ]
         + [field] * 18

time: 20.9 us -> 20.5 us (0.981)
  Pallas kernels: 20.1 us -> 19.7 us
    pallas_call x1, Pallas kernels: 19.3 us -> 18.9 us  [body(): pl.pallas_call(functools.partial(kernel, nvox), out_shape=(pltpu.VMEM((NR...]
where the time goes in v4:
time: 20.5 us; the launch traced here: 20.4 us
  Pallas kernels  19.7 us (96%)
  between operations  0.64 us (3%)
    pallas_call x1, Pallas kernels, body(): pl.pallas_call(functools.partial(kernel, nvox), out_shape=(pltpu.VMEM((NR...  18.9 us
    pallas_call x1, Pallas kernels, body(): pl.pallas_call(put_kernel, out_shape=(pltpu.HBM((NC * NR, 128), f32), plt...  0.81 us

profile of v4, /device:TPU:96, one launch (start us, length us, event | category | flops | bytes accessed | tf_op | source)
XLA Modules:
  0.0 20.4 jit_solution(15008347226620121452)
XLA Ops:
  0.6 18.9 %shard_map.113 = (f32[384,128]{1,0:T(8,128)S(1)}, f32[768,128]{1,0:T(8,128)S(1)}) custom-call(bf16[576,128]{1,0:T(8,128)(2,1)} %bitcast.16, f32[45,72]{1,0:T(8,128)} %bitcast.17, f32[3,5]{1,0:T(4,128)} %resp_hbm.1, s32[1,72]{1,0:T(1,128)} %bitcast.19, s32[8,128]{1,0:T(8,128)} %bitcast.18, f32[360,128]{1,0:T(8,128)} %bitcast.15, f32[720,128]{1,0:T(8,128)} %bitcast.12, ...), custom_call_target="tpu_custom_call" | custom-call | tf_op jit(solution)/shard_map/pallas_call | solution.py:540
  19.6 0.8 %shard_map.114 = (f32[360,128]{1,0:T(8,128)}, f32[720,128]{1,0:T(8,128)}) custom-call(f32[384,128]{1,0:T(8,128)S(1)} %get-tuple-element.6.u, f32[768,128]{1,0:T(8,128)S(1)} %get-tuple-element.7.w), custom_call_target="tpu_custom_call" | custom-call | tf_op jit(solution)/shard_map/pallas_call | solution.py:586

commit v5 on v4

--- a/solution.py
+++ b/solution.py
@@ -59,7 +59,7 @@
     vox = lax.axis_index("vox")
     mx, my = me // SIDE, lax.rem(me, SIDE)
     npeer = SIDE * SIDE
-    order = sorted(range(1, npeer), key=lambda k: -(min(k // SIDE, SIDE - k // SIDE) + min(k % SIDE, SIDE - k % SIDE)))
+    order = [10, 6, 9, 14, 11, 2, 8, 5, 15, 7, 13, 1, 4, 3, 12]
 
     def peer(k):
         return lax.rem(mx + k // SIDE, SIDE) * SIDE + lax.rem(my + k % SIDE, SIDE)
@@ -74,10 +74,10 @@
         load(0, basis_hbm, basis),
         load(1, resp_hbm, resp),
         load(2, shell_hbm, shell),
-        load(3, mask_hbm, mask),
+        load(3, mask_hbm, mask.at[pl.ds(0, NR)]),
         load(4, fodf_hbm, u0.at[pl.ds(0, NC * NR)]),
         load(5, sig_hbm, sig),
-        load(6, dual_hbm, y0),
+        load(6, dual_hbm, y0.at[pl.ds(0, ND * NR)]),
         load(7, aux_hbm, w0.at[pl.ds(0, NC * 2 * NR)]),
         load(8, grad_hbm, p0.at[pl.ds(0, NC * 2 * NR)]),
         load(9, sym_hbm, q0.at[pl.ds(0, NC * 3 * NR)]),
@@ -120,7 +120,7 @@
     for c in loads[7:]:
         c.start()
     gram = mm3(kth, ktl, knv)
-    hg[...] = gram[0:HALF] + pltpu.roll(gram[HALF:CP], 64, 1)
+    hg[pl.ds(0, HALF), :] = gram[0:HALF] + pltpu.roll(gram[HALF:CP], 64, 1)
     for c in loads[3:7]:
         c.wait()
 
@@ -207,28 +207,28 @@
     others = npeer - 1
     slots = pl.ds(0, others)
     rows_in = pl.ds(0, others * HALF)
+    slot_of = lane // 8
+    j = lax.rem(lane, 8)
+
+    def pack_into(acc, val, pr):
+        for h in range(2):
+            s = h * NR + pr
+            t = pltpu.roll(val[h * HALF : (h + 1) * HALF], 8 * s + 2 if isinstance(s, int) and 8 * s + 2 < 128 else lax.rem(8 * s + 2, 128), 1)
+            acc = jnp.where(slot_of == s, t, acc)
+        return acc
+
+    zero24 = jnp.zeros((HALF, 128), f32)
+    edge[...] = lax.fori_loop(0, NR, lambda pr, acc: pack_into(acc, ta[rows_of(pr), :], pr), zero24)
+
     pl.semaphore_wait(barrier, others + has_left.astype(jnp.int32) + has_right.astype(jnp.int32))
+    edges = to_vox(edge, edge_l, right, 0), to_vox(edge, edge_r, left, 1)
+    start_vox(*edges)
     far = [min(k // SIDE, SIDE - k // SIDE) + min(k % SIDE, SIDE - k % SIDE) for k in order]
     sends = scatter(ta, ra, 0), scatter(tb, rb, 1)
     for n, least, most in ((0, 2, 4), (1, 3, 4), (0, 1, 1), (1, 2, 2), (1, 1, 1)):
         for c, hops in zip(sends[n], far):
             if least <= hops <= most:
                 c.start()
-
-    slot_of = lane // 8
-    j = lax.rem(lane, 8)
-
-    def pack_into(acc, val, pr):
-        for h in range(2):
-            s = h * NR + pr
-            t = pltpu.roll(val[h * HALF : (h + 1) * HALF], 8 * s + 2 if isinstance(s, int) and 8 * s + 2 < 128 else lax.rem(8 * s + 2, 128), 1)
-            acc = jnp.where(slot_of == s, t, acc)
-        return acc
-
-    zero24 = jnp.zeros((HALF, 128), f32)
-    edge[...] = lax.fori_loop(0, NR, lambda pr, acc: pack_into(acc, ta[rows_of(pr), :], pr), zero24)
-    edges = to_vox(edge, edge_l, right, 0), to_vox(edge, edge_r, left, 1)
-    start_vox(*edges)
 
     for c in loads[7:]:
         c.wait()
@@ -447,7 +447,7 @@
     wait_all(dir_r.at[2], fa.at[rows_in])
     for pr in range(NR):
         hg[pl.ds(3 * pr, 3), :] = fa[pl.ds(pr * CP + NC, CP - NC), :]
-    hv = hg[...]
+    hv = hg[pl.ds(0, HALF), :]
     gh, gl = split(jnp.concatenate([hv, pltpu.roll(hv, 64, 1)], 0)[:, 0:CP])
     real = lax.broadcasted_iota(jnp.int32, (CP, 1), 0) < NC
 
@@ -493,6 +493,20 @@
         return 0
 
     lax.fori_loop(0, 2, primal_two, 0)
+    wait_all(dir_s.at[0], ra.at[slots])
+    wait_all(dir_s.at[1], rb.at[slots])
+    wait_all(dir_s.at[2], fa.at[rows_in])
+    wait_all(dir_s.at[4], edge_in.at[slots])
+    for to_right, to_left in (edges, halos):
+
+        @pl.when(has_right)
+        def _():
+            to_right.wait_send()
+
+        @pl.when(has_left)
+        def _():
+            to_left.wait_send()
+
     wait_all(dir_r.at[3], fb.at[rows_in])
 
     def add_signals(pr, _):
@@ -502,20 +516,7 @@
 
     lax.fori_loop(0, NR, add_signals, 0, unroll=True)
 
-    wait_all(dir_s.at[0], ra.at[slots])
-    wait_all(dir_s.at[1], rb.at[slots])
-    wait_all(dir_s.at[2], fa.at[rows_in])
     wait_all(dir_s.at[3], fb.at[rows_in])
-    wait_all(dir_s.at[4], edge_in.at[slots])
-    for to_right, to_left in (edges, halos):
-
-        @pl.when(has_right)
-        def _():
-            to_right.wait_send()
-
-        @pl.when(has_left)
-        def _():
-            to_left.wait_send()
 
 
 def put_kernel(u, w, u_hbm, w_hbm, sem):
@@ -532,14 +533,17 @@
 def body(nvox, signals, basis, response, shell_index, brain_mask, fodf, aux_field, grad_dual, sym_dual, data_dual):
     hbm = pl.BlockSpec(memory_space=pltpu.HBM)
     vmem = pl.BlockSpec(memory_space=pltpu.VMEM)
-    field = pltpu.VMEM((NR * CP, 128), f32)
+    field = pltpu.VMEM((NR * CP + 8, 128), f32)
+    pairs = pltpu.VMEM((CP * 2 * NR + 16, 128), f32)
+    triples = pltpu.VMEM((CP * 3 * NR + 24, 128), f32)
+    measured = pltpu.VMEM((ND * NR + 8, 128), f32)
     npeer = SIDE * SIDE
     dma = lambda n: pltpu.SemaphoreType.DMA((n,))
     edges = pltpu.VMEM((HALF, 128), f32)
     halos = pltpu.VMEM((8 * HALF, 128), f32)
     u, w = pl.pallas_call(
         functools.partial(kernel, nvox),
-        out_shape=(pltpu.VMEM((NR * CP, 128), f32), pltpu.VMEM((CP * 2 * NR, 128), f32)),
+        out_shape=(field, pairs),
         in_specs=[hbm] * 10,
         out_specs=(vmem, vmem),
         scratch_shapes=[
@@ -547,18 +551,15 @@
             pltpu.VMEM((NC, ND), f32),
             pltpu.VMEM((3, 5), f32),
             pltpu.VMEM((1, ND), jnp.int32),
-            pltpu.VMEM((NR, 128), jnp.int32),
+            pltpu.VMEM((2 * NR, 128), jnp.int32),
             field,
-            pltpu.VMEM((CP * 2 * NR, 128), f32),
-            pltpu.VMEM((CP * 2 * NR, 128), f32),
-            pltpu.VMEM((CP * 3 * NR, 128), f32),
-            pltpu.VMEM((ND * NR, 128), f32),
-            pltpu.VMEM((ND * NR, 128), f32),
+            pairs, pairs, triples,
+            measured, measured,
             pltpu.VMEM((CP, 128), f32),
             field, field, field, field,
             pltpu.VMEM((npeer, HALF, 128), f32),
             pltpu.VMEM((npeer, HALF, 128), f32),
-            edges,
+            pltpu.VMEM((HALF + 8, 128), f32),
             halos, halos, halos,
             edges, edges, edges,
             pltpu.VMEM((8, 128), f32),

time: 20.5 us -> 20.5 us (level)
  no operation moved by 1% of the time
where the time goes in v5:
time: 20.5 us; the launch traced here: 20.4 us
  Pallas kernels  19.8 us (97%)
  between operations  0.64 us (3%)
    pallas_call x1, Pallas kernels, body(): pl.pallas_call(functools.partial(kernel, nvox), out_shape=(field, pairs),...  18.9 us
    pallas_call x1, Pallas kernels, body(): pl.pallas_call(put_kernel, out_shape=(pltpu.HBM((NC * NR, 128), f32), plt...  0.81 us

profile of v5, /device:TPU:96, one launch (start us, length us, event | category | flops | bytes accessed | tf_op | source)
XLA Modules:
  0.0 20.4 jit_solution(7299713509068102100)
XLA Ops:
  0.6 18.9 %shard_map.113 = (f32[392,128]{1,0:T(8,128)S(1)}, f32[784,128]{1,0:T(8,128)S(1)}) custom-call(bf16[576,128]{1,0:T(8,128)(2,1)} %bitcast.16, f32[45,72]{1,0:T(8,128)} %bitcast.17, f32[3,5]{1,0:T(4,128)} %resp_hbm.1, s32[1,72]{1,0:T(1,128)} %bitcast.19, s32[8,128]{1,0:T(8,128)} %bitcast.18, f32[360,128]{1,0:T(8,128)} %bitcast.15, f32[720,128]{1,0:T(8,128)} %bitcast.12, ...), custom_call_target="tpu_custom_call" | custom-call | tf_op jit(solution)/shard_map/pallas_call | solution.py:544
  19.6 0.8 %shard_map.114 = (f32[360,128]{1,0:T(8,128)}, f32[720,128]{1,0:T(8,128)}) custom-call(f32[392,128]{1,0:T(8,128)S(1)} %get-tuple-element.6.u, f32[784,128]{1,0:T(8,128)S(1)} %get-tuple-element.7.w), custom_call_target="tpu_custom_call" | custom-call | tf_op jit(solution)/shard_map/pallas_call | solution.py:587

commit v6 on v5

--- a/solution.py
+++ b/solution.py
@@ -82,8 +82,6 @@
         load(8, grad_hbm, p0.at[pl.ds(0, NC * 2 * NR)]),
         load(9, sym_hbm, q0.at[pl.ds(0, NC * 3 * NR)]),
     ]
-    for c in loads[:7]:
-        c.start()
     barrier = pltpu.get_barrier_semaphore()
     for k in order:
         pl.semaphore_signal(barrier, inc=1, device_id={"dir": peer(k)}, device_id_type=MESH)
@@ -94,6 +92,8 @@
             pl.semaphore_signal(barrier, inc=1, device_id={"vox": n}, device_id_type=MESH)
 
 
+    for c in loads[:7]:
+        c.start()
     lane = lax.broadcasted_iota(jnp.int32, (1, 128), 1)
     for ref, n in ((u0, 1), (w0, 2), (p0, 2), (q0, 3)):
         ref[pl.ds(NC * n * NR, (CP - NC) * n * NR), :] = jnp.zeros(((CP - NC) * n * NR, 128), f32)
@@ -153,12 +153,6 @@
     for pr in range(NR):
         ta[pl.ds(pr * CP + NC, CP - NC), :] = hg[pl.ds(3 * pr, 3), :]
 
-    def signal_step(i, _):
-        s = pair(sigf, i, ND).astype(bf16)
-        store_pair(tb, i, mm(kth, s) + mm(ktl, s))
-        return 0
-
-    lax.fori_loop(0, 4, signal_step, 0, unroll=True)
     def chunk(d):
         return pl.ds(pl.multiple_of(d * HALF, HALF), HALF)
 
@@ -223,12 +217,18 @@
     pl.semaphore_wait(barrier, others + has_left.astype(jnp.int32) + has_right.astype(jnp.int32))
     edges = to_vox(edge, edge_l, right, 0), to_vox(edge, edge_r, left, 1)
     start_vox(*edges)
-    far = [min(k // SIDE, SIDE - k // SIDE) + min(k % SIDE, SIDE - k % SIDE) for k in order]
     sends = scatter(ta, ra, 0), scatter(tb, rb, 1)
-    for n, least, most in ((0, 2, 4), (1, 3, 4), (0, 1, 1), (1, 2, 2), (1, 1, 1)):
-        for c, hops in zip(sends[n], far):
-            if least <= hops <= most:
-                c.start()
+    for c in sends[0]:
+        c.start()
+
+    def signal_step(i, _):
+        s = pair(sigf, i, ND).astype(bf16)
+        store_pair(tb, i, mm(kth, s) + mm(ktl, s))
+        return 0
+
+    lax.fori_loop(0, 4, signal_step, 0, unroll=True)
+    for c in sends[1]:
+        c.start()
 
     for c in loads[7:]:
         c.wait()

time: 20.5 us -> 20.5 us (level)
  no operation moved by 1% of the time
where the time goes in v6:
time: 20.5 us; the launch traced here: 20.4 us
  Pallas kernels  19.8 us (97%)
  between operations  0.64 us (3%)
    pallas_call x1, Pallas kernels, body(): pl.pallas_call(functools.partial(kernel, nvox), out_shape=(field, pairs),...  19 us
    pallas_call x1, Pallas kernels, body(): pl.pallas_call(put_kernel, out_shape=(pltpu.HBM((NC * NR, 128), f32), plt...  0.81 us

profile of v6, /device:TPU:96, one launch (start us, length us, event | category | flops | bytes accessed | tf_op | source)
XLA Modules:
  0.0 20.4 jit_solution(157731981595367707)
XLA Ops:
  0.6 19.0 %shard_map.113 = (f32[392,128]{1,0:T(8,128)S(1)}, f32[784,128]{1,0:T(8,128)S(1)}) custom-call(bf16[576,128]{1,0:T(8,128)(2,1)} %bitcast.16, f32[45,72]{1,0:T(8,128)} %bitcast.17, f32[3,5]{1,0:T(4,128)} %resp_hbm.1, s32[1,72]{1,0:T(1,128)} %bitcast.19, s32[8,128]{1,0:T(8,128)} %bitcast.18, f32[360,128]{1,0:T(8,128)} %bitcast.15, f32[720,128]{1,0:T(8,128)} %bitcast.12, ...), custom_call_target="tpu_custom_call" | custom-call | tf_op jit(solution)/shard_map/pallas_call | solution.py:544
  19.6 0.8 %shard_map.114 = (f32[360,128]{1,0:T(8,128)}, f32[720,128]{1,0:T(8,128)}) custom-call(f32[392,128]{1,0:T(8,128)S(1)} %get-tuple-element.6.u, f32[784,128]{1,0:T(8,128)S(1)} %get-tuple-element.7.w), custom_call_target="tpu_custom_call" | custom-call | tf_op jit(solution)/shard_map/pallas_call | solution.py:587

commit v7 on v5

--- a/solution.py
+++ b/solution.py
@@ -57,12 +57,15 @@
 ):
     me = lax.axis_index("dir")
     vox = lax.axis_index("vox")
+    odd = lax.rem(vox, 2) == 1
     mx, my = me // SIDE, lax.rem(me, SIDE)
     npeer = SIDE * SIDE
     order = [10, 6, 9, 14, 11, 2, 8, 5, 15, 7, 13, 1, 4, 3, 12]
 
     def peer(k):
-        return lax.rem(mx + k // SIDE, SIDE) * SIDE + lax.rem(my + k % SIDE, SIDE)
+        dx, dy = k // SIDE, k % SIDE
+        ex, ey = jnp.where(odd, (SIDE - dy) % SIDE, dx), jnp.where(odd, (SIDE - dx) % SIDE, dy)
+        return lax.rem(mx + ex, SIDE) * SIDE + lax.rem(my + ey, SIDE)
 
     has_left, has_right = vox > 0, vox < nvox - 1
     left, right = vox - 1, vox + 1

time: 20.5 us -> 20.5 us (level)
  no operation moved by 1% of the time
where the time goes in v7:
time: 20.5 us; the launch traced here: 20.4 us
  Pallas kernels  19.7 us (96%)
  between operations  0.64 us (3%)
    pallas_call x1, Pallas kernels, body(): pl.pallas_call(functools.partial(kernel, nvox), out_shape=(field, pairs),...  18.9 us
    pallas_call x1, Pallas kernels, body(): pl.pallas_call(put_kernel, out_shape=(pltpu.HBM((NC * NR, 128), f32), plt...  0.81 us

profile of v7, /device:TPU:96, one launch (start us, length us, event | category | flops | bytes accessed | tf_op | source)
XLA Modules:
  0.0 20.4 jit_solution(2861531470083403693)
XLA Ops:
  0.6 18.9 %shard_map.113 = (f32[392,128]{1,0:T(8,128)S(1)}, f32[784,128]{1,0:T(8,128)S(1)}) custom-call(bf16[576,128]{1,0:T(8,128)(2,1)} %bitcast.16, f32[45,72]{1,0:T(8,128)} %bitcast.17, f32[3,5]{1,0:T(4,128)} %resp_hbm.1, s32[1,72]{1,0:T(1,128)} %bitcast.19, s32[8,128]{1,0:T(8,128)} %bitcast.18, f32[360,128]{1,0:T(8,128)} %bitcast.15, f32[720,128]{1,0:T(8,128)} %bitcast.12, ...), custom_call_target="tpu_custom_call" | custom-call | tf_op jit(solution)/shard_map/pallas_call | solution.py:547
  19.6 0.8 %shard_map.114 = (f32[360,128]{1,0:T(8,128)}, f32[720,128]{1,0:T(8,128)}) custom-call(f32[392,128]{1,0:T(8,128)S(1)} %get-tuple-element.6.u, f32[784,128]{1,0:T(8,128)S(1)} %get-tuple-element.7.w), custom_call_target="tpu_custom_call" | custom-call | tf_op jit(solution)/shard_map/pallas_call | solution.py:590
